TPU v7x, 256 devices: a whole 4x4x8 slice. The times are simulated.
256 devices in a mesh: leaf: 128 (over x, z, y), top: 2 (over core).
Axes of the slice: x: 4, y: 4, z: 8, core: 2. Of those that a mesh axis runs over, the one named last changes fastest.
Arguments:
- leaf_multipoles: bfloat16 [121, 32768], P(None, ('leaf', 'top')), may hold values from -6 to 6
- upward_ops: bfloat16 [121, 968], replicated, may hold values from -0.1875 to 0.1875
- transfer_ops: bfloat16 [121, 38236], replicated, may hold values from -0.046875 to 0.046875
- downward_ops: bfloat16 [121, 968], replicated, may hold values from -0.5 to 0.5
- send_lists: int32 [256, 128, 16], P(('leaf', 'top')), may hold values from 0 to 128, as said below
- leaf_pairs: int32 [316, 32768], P(None, 'leaf'), may hold values from 0 to 4352, as said below
- top_pairs: int32 [316, 4096], P(None, 'leaf'), may hold values from 0 to 4096, as said below
Outputs:
- leaf_locals: float32 [121, 32768], P(None, ('leaf', 'top'))
Inputs may be any that keep to these rules, and one draw needn't show every extreme that they name: send_lists[b, i, s] is a leaf cell of block b, counted within the block; 128 marks an unused slot. Used slots come before unused ones, cells in one list are distinct, and a block sends nothing to its own chip. leaf_pairs[c, t] is a column of the source table of the chip holding t, or 4352 where class c has no source; columns of unused received slots never appear. top_pairs[c, q] is a coarse cell, or 4096 where class c has no source.
All inputs are finite; a program needn't handle non-finite values.
Results may differ from a plain program's by a relative error of at most 0.0029.
Values may be sent and summed in bfloat16 or wider, within the bound.
No kernel may reach another device: no remote copies, remote signals or barrier semaphores. Data moves between devices by JAX's collectives and lax.ppermute only.
A program may use at most 128 MiB of HBM per device.

v0:
```python
import jax
import jax.numpy as jnp
from jax import lax
from jax.sharding import PartitionSpec as P

class_groups = 4


def with_zero(source_table):
    return jnp.concatenate(
        [source_table, jnp.zeros((source_table.shape[0], 1), source_table.dtype)], axis=1
    )


def padded_width(order_terms):
    return (order_terms + 127) // 128 * 128


def row_table(source_table):
    order_terms = source_table.shape[0]
    width = padded_width(order_terms)
    return jnp.pad(with_zero(source_table).T, ((0, 0), (0, width - order_terms)))


def prepare_ops(operators, order_terms):
    class_count = operators.shape[1] // order_terms
    width = padded_width(order_terms)
    arranged = operators.reshape(order_terms, class_count, order_terms).transpose(1, 0, 2)
    return jnp.pad(arranged, ((0, 0), (0, width - order_terms), (0, 0)))


def translate(source_rows, pair_lists, prepared):
    order_terms = prepared.shape[2]
    per_group = pair_lists.shape[0] // class_groups
    summed = jnp.zeros((order_terms, pair_lists.shape[1]), jnp.float32)
    for group_index in range(class_groups):
        first_class = group_index * per_group
        picked = jnp.take(source_rows, pair_lists[first_class : first_class + per_group], axis=0)
        operator_block = prepared[first_class : first_class + per_group]
        summed = summed + jnp.einsum(
            "cio,cti->ot", operator_block, picked, preferred_element_type=jnp.float32
        )
    return summed


def per_device(
    leaf_multipoles, upward_ops, transfer_ops, downward_ops, send_lists, leaf_pairs, top_pairs
):
    order_terms, cell_count = leaf_multipoles.shape
    core_index = lax.axis_index("top")
    coarse_count = cell_count // 8
    prepared = prepare_ops(transfer_ops, order_terms)
    padded = with_zero(leaf_multipoles)
    outgoing = jnp.take(padded, send_lists[0].reshape(-1), axis=1)
    arrived = lax.all_to_all(outgoing, "leaf", split_axis=1, concat_axis=1, tiled=True)
    children = leaf_multipoles.reshape(order_terms, coarse_count, 8)
    upward = upward_ops.reshape(order_terms, 8, order_terms)
    coarse_multi = jnp.einsum(
        "iko,iqk->oq", upward, children, preferred_element_type=jnp.float32
    ).astype(jnp.bfloat16)
    every_coarse = lax.all_gather(coarse_multi, ("leaf", "top"), axis=1, tiled=True)
    own_pairs = lax.dynamic_slice_in_dim(top_pairs, core_index * coarse_count, coarse_count, 1)
    coarse_local = translate(row_table(every_coarse), own_pairs, prepared)
    downward = downward_ops.reshape(order_terms, 8, order_terms)
    from_coarse = jnp.einsum(
        "iko,iq->oqk",
        downward,
        coarse_local.astype(jnp.bfloat16),
        preferred_element_type=jnp.float32,
    )
    from_coarse = from_coarse.reshape(order_terms, cell_count)
    both_cells, all_arrived = (
        lax.all_gather(leaf_multipoles, "top", axis=1, tiled=True),
        lax.all_gather(arrived, "top", axis=1, tiled=True),
    )
    source_rows = row_table(jnp.concatenate([both_cells, all_arrived], axis=1))
    own_pairs = lax.dynamic_slice_in_dim(leaf_pairs, core_index * cell_count, cell_count, 1)
    near_local = translate(source_rows, own_pairs, prepared)
    return near_local + from_coarse


def solution(mesh):
    in_specs = (
        P(None, ("leaf", "top")),
        P(),
        P(),
        P(),
        P(("leaf", "top"), None, None),
        P(None, "leaf"),
        P(None, "leaf"),
    )
    out_specs = P(None, ("leaf", "top"))
    return jax.shard_map(
        per_device, mesh=mesh, in_specs=in_specs, out_specs=out_specs, check_vma=False
    )
```

profile of v0, /device:TPU:1, one launch (start us, length us, event | category | flops | bytes accessed | tf_op | source)
XLA Modules:
  0.0 237.2 jit_solution(18404010383488999909)
XLA Ops:
  0.0 0.8 copy.24
  0.8 0.7 compare_and_fusion.8
  1.5 0.9 copy.21
  2.6 6.2 %gather_fusion = bf16[2048,121]{1,0:T(8,128)(2,1)S(1)} fusion(bf16[121,129]{0,1:T(8,128)(2,1)S(1)} %concatenate.9, s32[2048]{0:T(1024)S(1)} %broadcast_clamp_fusion), kind=kCustom, calls=%fused_computation.8 | custom fusion | bytes 999424 | tf_op jit(solution)/shard_map/jit(_take)/gather | solution.py:54
  8.8 1.1 broadcast_select_fusion
  10.0 16.3 %all-to-all-start = ((bf16[121,128,16]{0,2,1:T(8,128)(2,1)}), bf16[121,128,16]{0,2,1:T(8,128)(2,1)S(1)}, u32[]{:S(2)}, u32[]{:S(2)}) async-start(bf16[121,128,16]{0,2,1:T(8,128)(2,1)} %broadcast_select_fusion), calls=%async_computation | async-start | bytes 1048576 | tf_op jit(solution)/shard_map/all_to_all | solution.py:55
  26.4 14.3 %reshape.202 = bf16[121,316,121]{0,2,1:T(8,128)(2,1)} reshape(bf16[121,38236]{0,1:T(8,128)(2,1)} %param.13) | data formatting | bytes 18506224 | tf_op jit(solution)/shard_map/reshape | solution.py:28
  41.0 0.2 fusion.92
  41.2 64.3 %all_gather.11 = bf16[121,4096]{0,1:T(8,128)(2,1)S(1)} all-gather(bf16[121,16]{0,1:T(8,128)(2,1)S(1)} %fusion.92), channel_id=1, replica_groups=mesh['leaf'=128,'top'=2] {'leaf','top'}, dimensions={1}, use_global_device_ids=true | all-gather | bytes 995104 | tf_op jit(solution)/shard_map/all_gather | solution.py:61
  105.5 0.2 pad_bitcast_fusion
  105.7 0.2 pad.16
  106.2 3.0 %gather_fusion.5 = bf16[1264,128]{1,0:T(8,128)(2,1)S(1)} fusion(bf16[4097,128]{1,0:T(8,128)(2,1)S(1)} %pad.16, s32[2048]{0:T(1024)S(1)} %pad_clamp_fusion.7), kind=kCustom, calls=%fused_computation.1.clone | custom fusion | bytes 652224 | tf_op jit(solution)/shard_map/jit(_take)/gather | solution.py:38
  109.2 3.0 %gather_fusion.6 = bf16[1264,128]{1,0:T(8,128)(2,1)S(1)} fusion(bf16[4097,128]{1,0:T(8,128)(2,1)S(1)} %pad.16, s32[2048]{0:T(1024)S(1)} %pad_clamp_fusion.6), kind=kCustom, calls=%fused_computation.5.clone | custom fusion | bytes 652224 | tf_op jit(solution)/shard_map/jit(_take)/gather | solution.py:38
  112.6 3.0 %gather_fusion.7 = bf16[1264,128]{1,0:T(8,128)(2,1)S(1)} fusion(bf16[4097,128]{1,0:T(8,128)(2,1)S(1)} %pad.16, s32[2048]{0:T(1024)S(1)} %pad_clamp_fusion.5), kind=kCustom, calls=%fused_computation.6.clone | custom fusion | bytes 652224 | tf_op jit(solution)/shard_map/jit(_take)/gather | solution.py:38
  115.9 3.0 %gather_fusion.8 = bf16[1264,128]{1,0:T(8,128)(2,1)S(1)} fusion(bf16[4097,128]{1,0:T(8,128)(2,1)S(1)} %pad.16, s32[2048]{0:T(1024)S(1)} %pad_clamp_fusion.4), kind=kCustom, calls=%fused_computation.7.clone | custom fusion | bytes 652224 | tf_op jit(solution)/shard_map/jit(_take)/gather | solution.py:38
  119.1 2.7 %fusion.68 = f32[121,16]{0,1:T(8,128)S(1)} fusion(bf16[316,121,121]{1,2,0:T(8,128)(2,1)} %bitcast.89, bf16[79,16,128]{2,1,0:T(8,128)(2,1)S(1)} %bitcast.107, pred[79,16]{1,0:T(8,128)(4,1)S(1)} %copy.25), kind=kOutput, calls=%fused_computation.47 | convolution fusion | flops 39315456 | bytes 9585704 | tf_op jit(solution)/shard_map/cio,cti->ot/dot_general | solution.py:40
  121.8 3.1 %fusion.86 = f32[121,16]{0,1:T(8,128)S(1)} fusion(f32[121,16]{0,1:T(8,128)S(1)} %fusion.68, bf16[316,121,121]{1,2,0:T(8,128)(2,1)} %bitcast.90, bf16[79,16,128]{2,1,0:T(8,128)(2,1)S(1)} %bitcast.109, pred[79,16]{1,0:T(8,128)(4,1)S(1)} %copy.31), kind=kOutput, calls=%fused_computation.54 | convolution fusion | flops 39317392 | bytes 9593448 | tf_op jit(solution)/shard_map/cio,cti->ot/dot_general | solution.py:40
  124.9 0.8 fusion.83
  125.8 2.8 %convolution_bitcast_fusion = f32[121,16,8]{0,1,2:T(8,128)S(1)} fusion(bf16[121,8,121]{0,2,1:T(8,128)(2,1)S(1)} %reshape.204, f32[121,16]{0,1:T(8,128)S(1)} %fusion.83, bf16[316,121,121]{1,2,0:T(8,128)(2,1)} %bitcast.91, bf16[79,16,128]{2,1,0:T(8,128)(2,1)S(1)} %bitcast.108, pred[79,16]{1,0:T(8,128)(4,1)S(1)} %copy.35), kind=kOutput, calls=%fused_computation.41 | convolution fusion | flops 43067424 | bytes 9881912 | tf_op jit(solution)/shard_map/iko,iq->oqk/dot_general | solution.py:65
  128.7 1.9 all_gather.9
  130.9 2.7 %all_gather.10 = bf16[121,4096]{0,1:T(8,128)(2,1)S(1)} all-gather(bf16[121,2048]{0,1:T(8,128)(2,1)S(1)} %bitcast.105), channel_id=1, replica_groups=mesh['leaf'=128,'top'=2] {'top'}, dimensions={1}, use_global_device_ids=true | all-gather | bytes 1486848 | tf_op jit(solution)/shard_map/all_gather | solution.py:74
  133.6 2.6 %maximum_bitcast_fusion = bf16[4353,121]{1,0:T(8,128)(2,1)S(1)} fusion(bf16[121,4096]{0,1:T(8,128)(2,1)S(1)} %all_gather.10, bf16[121,256]{0,1:T(8,128)(2,1)S(1)} %all_gather.9, bf16[4353]{0:T(1024)(128)(2,1)S(1)} %pad.19.clone), kind=kLoop, calls=%fused_computation.46 | loop fusion | flops 3160278 | bytes 2115316 | tf_op jit(solution)/shard_map/transpose | solution.py:22
  136.3 0.2 pad.15
  136.5 21.3 %gather_fusion.1 = bf16[10112,128]{1,0:T(8,128)(2,1)} fusion(bf16[4353,128]{1,0:T(8,128)(2,1)S(1)} %pad.15, s32[10240]{0:T(1024)S(1)} %get-tuple-element.32), kind=kCustom, calls=%fused_computation.clone | custom fusion | bytes 5217792 | tf_op jit(solution)/shard_map/jit(_take)/gather | solution.py:38
  157.8 21.2 %gather_fusion.2 = bf16[10112,128]{1,0:T(8,128)(2,1)} fusion(bf16[4353,128]{1,0:T(8,128)(2,1)S(1)} %pad.15, s32[10240]{0:T(1024)S(1)} %get-tuple-element.31), kind=kCustom, calls=%fused_computation.2.clone | custom fusion | bytes 5217792 | tf_op jit(solution)/shard_map/jit(_take)/gather | solution.py:38
  179.0 21.3 %gather_fusion.3 = bf16[10112,128]{1,0:T(8,128)(2,1)} fusion(bf16[4353,128]{1,0:T(8,128)(2,1)S(1)} %pad.15, s32[10240]{0:T(1024)S(1)} %get-tuple-element.30), kind=kCustom, calls=%fused_computation.3.clone | custom fusion | bytes 5217792 | tf_op jit(solution)/shard_map/jit(_take)/gather | solution.py:38
  200.3 21.3 %gather_fusion.4 = bf16[10112,128]{1,0:T(8,128)(2,1)} fusion(bf16[4353,128]{1,0:T(8,128)(2,1)S(1)} %pad.15, s32[10240]{0:T(1024)S(1)} %get-tuple-element.29), kind=kCustom, calls=%fused_computation.4.clone | custom fusion | bytes 5217792 | tf_op jit(solution)/shard_map/jit(_take)/gather | solution.py:38
  221.6 5.4 %fusion.28 = f32[121,128]{1,0:T(8,128)S(1)} fusion(bf16[79,128,128]{2,1,0:T(8,128)(2,1)} %bitcast.103, pred[79,128]{1,0:T(8,128)(4,1)S(1)} %get-tuple-element.18, bf16[316,121,121]{1,2,0:T(8,128)(2,1)} %bitcast.92), kind=kOutput, calls=%fused_computation.37 | convolution fusion | flops 314523648 | bytes 11913848 | tf_op jit(solution)/shard_map/cio,cti->ot/dot_general | solution.py:40
  227.0 6.3 %fusion.63 = f32[121,128]{1,0:T(8,128)S(1)} fusion(f32[121,128]{1,0:T(8,128)S(1)} %fusion.28, bf16[79,128,128]{2,1,0:T(8,128)(2,1)S(1)} %bitcast.104, pred[79,128]{1,0:T(8,128)(4,1)S(1)} %get-tuple-element.17, bf16[316,121,121]{1,2,0:T(8,128)(2,1)} %bitcast.93), kind=kOutput, calls=%fused_computation.45 | convolution fusion | flops 314539136 | bytes 11975800 | tf_op jit(solution)/shard_map/cio,cti->ot/dot_general | solution.py:40
  233.3 1.6 fusion.58
  234.9 0.1 copy-done
  235.0 2.2 fusion.53
  (59 shorter events, 2.2 us)
Async XLA Ops:
  10.0 120.9 %all-to-all-start = ((bf16[121,128,16]{0,2,1:T(8,128)(2,1)}), bf16[121,128,16]{0,2,1:T(8,128)(2,1)S(1)}, u32[]{:S(2)}, u32[]{:S(2)}) async-start(bf16[121,128,16]{0,2,1:T(8,128)(2,1)} %broadcast_select_fusion), calls=%async_computation | async-start | bytes 1048576 | tf_op jit(solution)/shard_map/all_to_all | solution.py:55
  26.3 14.3 %copy-start.6 = (s32[316,32]{0,1:T(8,128)S(1)}, s32[316,32]{0,1:T(8,128)}, u32[]{:S(2)}) copy-start(s32[316,32]{0,1:T(8,128)} %param.17) | copy-start | bytes 121348
  26.3 14.6 %copy-start.4 = (bf16[121,968]{0,1:T(8,128)(2,1)S(1)}, bf16[121,968]{0,1:T(8,128)(2,1)}, u32[]{:S(2)}) copy-start(bf16[121,968]{0,1:T(8,128)(2,1)} %param.12) | copy-start | bytes 702772
  112.6 6.5 %copy-start.5 = (bf16[121,968]{0,1:T(8,128)(2,1)S(1)}, bf16[121,968]{0,1:T(8,128)(2,1)}, u32[]{:S(2)}) copy-start(bf16[121,968]{0,1:T(8,128)(2,1)} %param.14) | copy-start | bytes 702772
  119.1 5.8 %slice-start = ((s8[10354688]{0:T(1024)(128)(4,1)}), s8[4194304]{0:T(1024)(128)(4,1)S(1)}, s32[]{:S(2)}) async-start(s8[10354688]{0:T(1024)(128)(4,1)} %bitcast.94), calls=%async_computation.1 | async-start | bytes 8388608
  119.1 5.8 %slice-start.1 = ((s8[10354688]{0:T(1024)(128)(4,1)}), s8[4194304]{0:T(1024)(128)(4,1)S(1)}, s32[]{:S(2)}) async-start(s8[10354688]{0:T(1024)(128)(4,1)} %bitcast.94), calls=%async_computation.2 | async-start | bytes 8388608
  121.8 3.1 %slice-start.2 = ((s8[10354688]{0:T(1024)(128)(4,1)}), s8[1966080]{0:T(1024)(128)(4,1)S(1)}, s32[]{:S(2)}) async-start(s8[10354688]{0:T(1024)(128)(4,1)} %bitcast.94), calls=%async_computation.3 | async-start | bytes 3932160
  125.8 4.8 %copy-start.3 = (s32[316,256]{1,0:T(8,128)S(1)}, s32[316,256]{1,0:T(8,128)}, u32[]{:S(2)}) copy-start(s32[316,256]{1,0:T(8,128)} %param.16) | copy-start | bytes 970756
  221.6 5.4 %copy-start.2 = (bf16[10112,128]{1,0:T(8,128)(2,1)S(1)}, bf16[10112,128]{1,0:T(8,128)(2,1)}, u32[]{:S(2)}) copy-start(bf16[10112,128]{1,0:T(8,128)(2,1)} %gather_fusion.2) | copy-start | bytes 7766020
  221.6 11.7 %slice-start.3 = ((s8[10354688]{0:T(1024)(128)(4,1)}), s8[4194304]{0:T(1024)(128)(4,1)S(1)}, s32[]{:S(2)}) async-start(s8[10354688]{0:T(1024)(128)(4,1)} %bitcast.97), calls=%async_computation.4 | async-start | bytes 8388608
  221.6 11.7 %slice-start.4 = ((s8[10354688]{0:T(1024)(128)(4,1)}), s8[4194304]{0:T(1024)(128)(4,1)S(1)}, s32[]{:S(2)}) async-start(s8[10354688]{0:T(1024)(128)(4,1)} %bitcast.97), calls=%async_computation.5 | async-start | bytes 8388608
  227.0 6.3 %slice-start.5 = ((s8[10354688]{0:T(1024)(128)(4,1)}), s8[1966080]{0:T(1024)(128)(4,1)S(1)}, s32[]{:S(2)}) async-start(s8[10354688]{0:T(1024)(128)(4,1)} %bitcast.97), calls=%async_computation.6 | async-start | bytes 3932160
  227.0 6.3 %copy-start.1 = (bf16[10112,128]{1,0:T(8,128)(2,1)S(1)}, bf16[10112,128]{1,0:T(8,128)(2,1)}, u32[]{:S(2)}) copy-start(bf16[10112,128]{1,0:T(8,128)(2,1)} %gather_fusion.3) | copy-start | bytes 7766020
  233.3 1.7 copy-start
where the time goes:
time: 238 us; the launch traced here: 237 us
  local copies, waits for them, and re-layouts  122 us (51%)
  blocking collectives  68.9 us (29%)
  matrix products  24.9 us (10%)
  starting transfers between devices  16.3 us (7%)
  other arithmetic  4.9 us (2%)
    gather x8, local copies, waits for them, and re-layouts, translate(): jnp.take(source_rows, pair_lists[first_class:first_class + per_group], ax...  97.1 us
    all_gather x1, blocking collectives, per_device(): lax.all_gather(coarse_multi, ('leaf', 'top'), axis=1, tiled=True)  64.3 us
    dot_general x7, matrix products, translate(): jnp.einsum('cio,cti->ot', operator_block, picked, preferred_element_type=...  22 us
    all_to_all x1, starting transfers between devices, per_device(): lax.all_to_all(outgoing, 'leaf', split_axis=1, concat_axis=1, tiled=True)  16.3 us
    reshape x1, local copies, waits for them, and re-layouts, prepare_ops(): operators.reshape(order_terms, class_count, order_terms).transpose(1, 0, 2)  14.3 us
    gather x1, local copies, waits for them, and re-layouts, per_device(): outgoing = jnp.take(padded, send_lists[0].reshape(-1), axis=1)  6.18 us
  transfers between devices with their start and end apart: 1, of which 0 were waited for; matrix products, arithmetic and copies ran while one was open for 16% of the time, Pallas kernels for 0%

commit v1 on v0

v1 whole, which is shorter than its diff:
```python
import functools

import jax
import jax.numpy as jnp
from jax import lax
from jax.experimental import pallas as pl
from jax.experimental.pallas import tpu as pltpu
from jax.sharding import PartitionSpec as P

BF = jnp.bfloat16
F32 = jnp.float32
I32 = jnp.int32

WIDTH = 128
GROUP = 8
TILE = 512
HALF = TILE // 2
BLOCK = 128


def nt_dot(left, right):
    return lax.dot_general(
        left, right, (((1,), (1,)), ((), ())), preferred_element_type=F32
    )


def dot(left, right):
    return jnp.dot(left, right, preferred_element_type=F32)


def main_kernel(
    flag_lane,
    core_ref,
    coarse_pos,
    arrived,
    local_cells,
    pairs,
    operators,
    downward,
    keep,
    send,
    places,
    tables,
    coarse_rows,
    picked,
    near_sum,
    coarse_sum,
):
    core = core_ref[0]
    peers, rows_each, width = arrived.shape
    slots = rows_each // 2
    slot_count = peers * slots
    class_count, targets = pairs.shape
    groups = places.shape[0] // GROUP
    coarse_targets = coarse_sum.shape[1]
    local_count = local_cells.shape[1]

    received = arrived[:, :slots, :].reshape(slot_count, width)
    flag_pick = (lax.broadcasted_iota(I32, (16, width), 1) == flag_lane).astype(F32).astype(BF)
    flags = nt_dot(flag_pick, received)
    by_peer = (
        lax.broadcasted_iota(I32, (slot_count, peers), 0) // slots
        == lax.broadcasted_iota(I32, (slot_count, peers), 1)
    )
    counts = dot(flags.astype(BF), by_peer.astype(F32).astype(BF))
    before = (
        lax.broadcasted_iota(I32, (peers, peers), 0) < lax.broadcasted_iota(I32, (peers, peers), 1)
    )
    first = dot(counts.astype(BF), before.astype(F32).astype(BF))[:8].astype(I32) + local_count
    used = jnp.sum(counts[0:1, :]).astype(I32)
    tile_count = (local_count + used + TILE - 1) // TILE

    lane = lax.broadcasted_iota(I32, (8, peers), 1)
    dest_parts = []
    for part in range(slots):
        slot = lane + part * peers
        at = jnp.take_along_axis(first, slot // slots, axis=1) + slot % slots
        live = flags[:8, part * peers : (part + 1) * peers] > 0.5
        dest_parts.append(jnp.where(live, at, -1))
    dest = jnp.concatenate(dest_parts, axis=1)[0:1]

    def place(row, _):
        start = pl.multiple_of(row * 8, 8)
        inside = pairs[pl.ds(start, 8), :]
        places[pl.ds(start, 8), :] = place_rows(inside)
        return 0

    def place_rows(column):
        parts = []
        for half in range(targets // peers):
            col = column[:, half * peers : (half + 1) * peers]
            slot = col - 2 * local_count - core * slot_count
            mine = (slot >= 0) & (slot < slot_count)
            safe = jnp.where(mine, slot, 0)
            far = jnp.take_along_axis(first, safe // slots, axis=1) + safe % slots
            near = col - core * local_count
            parts.append(
                jnp.where(mine, far, jnp.where((near >= 0) & (near < local_count), near, -1))
            )
        return jnp.concatenate(parts, axis=1)

    whole = class_count // 8
    lax.fori_loop(0, whole, place, 0)
    tail = class_count - whole * 8
    if tail:
        rest = pairs[whole * 8 : class_count, :]
        rest = jnp.concatenate([rest, jnp.full((8 - tail, targets), 1 << 20, I32)], axis=0)
        places[whole * 8 : whole * 8 + 8, :] = place_rows(rest)

    def pack(tile, _):
        for part in range(TILE // peers):
            base = tile * TILE + part * peers
            one_hot = (
                lax.broadcasted_iota(I32, (peers, slot_count), 0) + base == dest
            ).astype(F32).astype(BF)
            cells = dot(one_hot, received).T.astype(BF)
            half, at = divmod(part * peers, HALF)
            tables[tile, half * width : (half + 1) * width, at : at + peers] = cells
        return 0

    lax.fori_loop(0, tile_count, pack, 0)
    tables[0, :width, :local_count] = local_cells[...]

    coarse_rows[:slot_count, :] = arrived[:, slots:, :].reshape(slot_count, width).astype(F32)
    coarse_rows[slot_count:, :] = jnp.zeros((8, width), F32)

    near_sum[...] = jnp.zeros_like(near_sum)
    coarse_sum[...] = jnp.zeros_like(coarse_sum)
    row_index = lax.broadcasted_iota(I32, (HALF, targets), 0)

    def gather(table, position):
        inside = (position >= 0) & (position < TILE)
        low = jnp.where(inside, position & (HALF - 1), -1)
        one_hot = jnp.where(row_index == low, 1.0, 0.0).astype(BF)
        both = dot(table, one_hot)
        return jnp.where(position >= HALF, both[width:], both[:width]).astype(BF)

    def near_step(table, group, base):
        position = places[pl.ds(pl.multiple_of(group * GROUP, GROUP), GROUP), :] - base
        total = near_sum[...]
        for pair in range(GROUP // 2):
            cells = jnp.concatenate(
                [gather(table, position[2 * pair + j : 2 * pair + j + 1]) for j in range(2)], axis=0
            )
            total = total + dot(operator_pair(group, pair), cells)
        near_sum[...] = total

    def operator_pair(group, pair):
        start = pl.multiple_of((group * GROUP + 2 * pair) * width, 2 * width)
        return operators[:, pl.ds(start, 2 * width)]

    def first_tile(group, _):
        base = group * (GROUP * coarse_targets)
        for row in range(GROUP * coarse_targets):
            picked[pl.ds(row, 1), :] = coarse_rows[pl.ds(coarse_pos[base + row], 1), :]
        near_step(tables[0], group, 0)
        total = coarse_sum[...]
        for pair in range(GROUP // 2):
            at = 2 * pair * coarse_targets
            cells = jnp.concatenate(
                [
                    picked[at + j * coarse_targets : at + (j + 1) * coarse_targets, :].astype(BF)
                    for j in range(2)
                ],
                axis=1,
            )
            total = total + nt_dot(operator_pair(group, pair), cells)
        coarse_sum[...] = total
        return 0

    lax.fori_loop(0, groups, first_tile, 0)

    def more_tiles(tile, _):
        table = tables[tile]

        def step(group, _):
            near_step(table, group, tile * TILE)
            return 0

        return lax.fori_loop(0, groups, step, 0)

    lax.fori_loop(1, tile_count, more_tiles, 0)

    children = targets // coarse_targets
    spread = (
        lax.broadcasted_iota(I32, (coarse_targets, targets), 1) // children
        == lax.broadcasted_iota(I32, (coarse_targets, targets), 0)
    ).astype(F32).astype(BF)
    child = lax.broadcasted_iota(I32, (width, targets), 1) % children
    total = near_sum[...]
    real = lax.broadcasted_iota(I32, (width, coarse_targets), 0) < flag_lane
    rest = jnp.where(real, coarse_sum[...], 0.0)
    for _ in range(2):
        term = rest.astype(BF)
        rest = rest - term.astype(F32)
        wide = dot(term, spread)
        stacked = jnp.concatenate(
            [jnp.where(child == k, wide, 0.0).astype(BF) for k in range(children)], axis=0
        )
        total = total + dot(downward[...], stacked)
    left, right = total[:, :local_count], total[:, local_count:]
    keep[...] = jnp.where(core == 0, left, right)
    send[...] = jnp.where(core == 0, right, left)


def arrange(operators, order_terms):
    class_count = operators.shape[1] // order_terms
    arranged = operators.reshape(order_terms, class_count, order_terms).transpose(2, 1, 0)
    pad = WIDTH - order_terms
    arranged = jnp.pad(arranged, ((0, pad), (0, 0), (0, pad)))
    return arranged.reshape(WIDTH, class_count * WIDTH)


def arrange_kernel(class_count, source, arranged, rows):
    lines, order_terms = source.shape
    step = pl.program_id(0)
    rows[:, order_terms:] = jnp.zeros((lines + 8, WIDTH - order_terms), F32)
    rows[lines:, :] = jnp.zeros((8, WIDTH), F32)

    def widen(block, _):
        start = pl.multiple_of(block * WIDTH, WIDTH)
        rows[pl.ds(start, WIDTH), :order_terms] = source[pl.ds(start, WIDTH), :].astype(F32)
        return 0

    lax.fori_loop(0, lines // WIDTH, widen, 0, unroll=4)

    def cut(index, _):
        start = pl.multiple_of(index * WIDTH, WIDTH)
        real = step * BLOCK + index < class_count
        square = jnp.where(real, rows[pl.ds(index * order_terms, WIDTH), :], 0.0)
        arranged[:, pl.ds(start, WIDTH)] = square.astype(BF)
        return 0

    lax.fori_loop(0, BLOCK, cut, 0, unroll=4)


def arrange_classes(operators, order_terms):
    class_count = operators.shape[0] // order_terms
    padded_count = (class_count + GROUP - 1) // GROUP * GROUP
    lines = BLOCK * order_terms
    steps = (class_count + BLOCK - 1) // BLOCK
    return pl.pallas_call(
        functools.partial(arrange_kernel, class_count),
        grid=(steps,),
        out_shape=jax.ShapeDtypeStruct((WIDTH, padded_count * WIDTH), BF),
        in_specs=[pl.BlockSpec((lines, order_terms), lambda step: (step, 0))],
        out_specs=pl.BlockSpec((WIDTH, BLOCK * WIDTH), lambda step: (0, step)),
        scratch_shapes=[pltpu.VMEM((lines + 8, WIDTH), F32)],
        compiler_params=pltpu.CompilerParams(vmem_limit_bytes=40 << 20),
        cost_estimate=pl.CostEstimate(
            flops=0, bytes_accessed=40 * 1024 * 1024, transcendentals=0
        ),
    )(operators)


def outgoing_kernel(cells, chosen, upward, outgoing, spread, risen):
    order_terms, cell_count = cells.shape
    slots, peers = chosen.shape
    coarse_count = cell_count // 8
    pad = WIDTH - order_terms
    values = cells[...].astype(F32)
    flag = (lax.broadcasted_iota(I32, (pad, cell_count), 0) == 0).astype(F32)
    flagged = jnp.concatenate([values, flag], axis=0).astype(BF)
    columns = jnp.concatenate(
        [chosen[...].astype(F32), jnp.zeros((peers - slots, peers), F32)], axis=0
    ).T.astype(I32)
    cell = lax.broadcasted_iota(I32, (peers, cell_count), 1)
    for slot in range(slots):
        one_hot = (cell == columns[:, slot : slot + 1]).astype(F32).astype(BF)
        spread[pl.ds(slot, peers, stride=slots), :] = nt_dot(one_hot, flagged)
    outgoing[:, :slots, :] = spread[...].astype(BF).reshape(peers, slots, WIDTH)

    risen[: 8 * order_terms, :] = dot(upward[...], cells[...])
    risen[8 * order_terms :, :] = jnp.zeros((8, cell_count), F32)
    child = lax.broadcasted_iota(I32, (WIDTH, cell_count), 1) % 8
    total = jnp.zeros((WIDTH, cell_count), F32)
    for k in range(8):
        total = total + jnp.where(child == k, risen[pl.ds(k * order_terms, WIDTH), :], 0.0)
    real = lax.broadcasted_iota(I32, (WIDTH, cell_count), 0) < order_terms
    total = jnp.where(real, total, 0.0).T
    coarse = jnp.sum(total.reshape(coarse_count, 8, WIDTH), axis=1).astype(BF)
    outgoing[:, slots:, :] = jnp.broadcast_to(coarse[None], (peers, coarse_count, WIDTH))


def per_device(
    leaf_multipoles, upward_ops, transfer_ops, downward_ops, send_lists, leaf_pairs, top_pairs
):
    order_terms, cell_count = leaf_multipoles.shape
    _, peers, slots = send_lists.shape
    class_count, targets = leaf_pairs.shape
    coarse_targets = top_pairs.shape[1]
    coarse_count = cell_count // 8
    core = lax.axis_index("top").astype(I32)
    vmem = pl.BlockSpec(memory_space=pltpu.VMEM)
    smem = pl.BlockSpec(memory_space=pltpu.SMEM)

    outgoing = pl.pallas_call(
        outgoing_kernel,
        out_shape=jax.ShapeDtypeStruct((peers, slots + coarse_count, WIDTH), BF),
        in_specs=[vmem] * 3,
        out_specs=vmem,
        scratch_shapes=[
            pltpu.VMEM((peers * slots, WIDTH), F32),
            pltpu.VMEM((8 * order_terms + 8, cell_count), F32),
        ],
        compiler_params=pltpu.CompilerParams(vmem_limit_bytes=16 << 20),
    )(leaf_multipoles, send_lists[0].T, upward_ops.T)
    arrived = lax.all_to_all(outgoing, "leaf", split_axis=0, concat_axis=0, tiled=True)

    local_cells = jnp.pad(leaf_multipoles, ((0, WIDTH - order_terms), (0, 0)))
    operators = arrange_classes(transfer_ops.T, order_terms)
    downward = arrange(downward_ops, order_terms)
    padded_classes = operators.shape[1] // WIDTH
    source_core = (top_pairs // coarse_count) % 2
    source_row = top_pairs // (2 * coarse_count) * coarse_count + top_pairs % coarse_count
    zero_row = peers * coarse_count
    held = (source_core == core) & (top_pairs < 2 * zero_row)
    coarse_pos = jnp.where(held, source_row, zero_row)
    coarse_pos = jnp.pad(
        coarse_pos, ((0, padded_classes - class_count), (0, 0)), constant_values=zero_row
    ).reshape(-1)

    most_tiles = (cell_count + peers * slots + TILE - 1) // TILE
    half_shape = jax.ShapeDtypeStruct((WIDTH, cell_count), F32)
    keep, send = pl.pallas_call(
        functools.partial(main_kernel, order_terms),
        out_shape=(half_shape, half_shape),
        in_specs=[smem, smem] + [vmem] * 5,
        out_specs=(vmem, vmem),
        scratch_shapes=[
            pltpu.VMEM((padded_classes, targets), I32),
            pltpu.VMEM((most_tiles, 2 * WIDTH, HALF), BF),
            pltpu.VMEM((zero_row + 8, WIDTH), F32),
            pltpu.VMEM((GROUP * coarse_targets, WIDTH), F32),
            pltpu.VMEM((WIDTH, targets), F32),
            pltpu.VMEM((WIDTH, coarse_targets), F32),
        ],
        compiler_params=pltpu.CompilerParams(vmem_limit_bytes=40 << 20),
    )(core.reshape(1), coarse_pos, arrived, local_cells, leaf_pairs, operators, downward)
    other = lax.ppermute(send, "top", [(0, 1), (1, 0)])
    return (keep + other)[:order_terms]


def solution(mesh):
    in_specs = (
        P(None, ("leaf", "top")),
        P(),
        P(),
        P(),
        P(("leaf", "top"), None, None),
        P(None, "leaf"),
        P(None, "leaf"),
    )
    out_specs = P(None, ("leaf", "top"))
    return jax.shard_map(
        per_device, mesh=mesh, in_specs=in_specs, out_specs=out_specs, check_vma=False
    )
```

time: 238 us -> 109 us (0.46)
  local copies, waits for them, and re-layouts: 122 us -> 12.5 us
  blocking collectives: 68.9 us -> 0 us
  Pallas kernels: 0 us -> 61.9 us
  matrix products: 24.9 us -> 0 us
  waiting for transfers between devices: 0.01 us -> 12.5 us
  starting transfers between devices: 16.3 us -> 20 us
  other arithmetic: 4.9 us -> 1.53 us
    gather x9 -> x0, local copies, waits for them, and re-layouts: 103 us -> none  [the longest x8 97.1 us: translate(): jnp.take(source_rows, pair_lists[first_class:first_class + per_group], ax...]
    all_gather x3 -> x0, blocking collectives: 68.9 us -> none  [the longest x1 64.3 us: per_device(): lax.all_gather(coarse_multi, ('leaf', 'top'), axis=1, tiled=True)]
    pallas_call x0 -> x3, Pallas kernels: none -> 61.9 us  [the longest x1 51.2 us: per_device(): pl.pallas_call(functools.partial(main_kernel, order_terms), out_shape=(ha...]
    dot_general x9 -> x0, matrix products: 24.9 us -> none  [the longest x7 22 us: translate(): jnp.einsum('cio,cti->ot', operator_block, picked, preferred_element_type=...]
    reshape x4 -> x2, local copies, waits for them, and re-layouts: 14.5 us -> 1.1 us  [the longest x1 1.01 us: arrange(): operators.reshape(order_terms, class_count, order_terms).transpose(2, 1, 0)]
    all_to_all x1, waiting for transfers between devices: 0.01 us -> 11.6 us  [per_device(): lax.all_to_all(outgoing, 'leaf', split_axis=0, concat_axis=0, tiled=True)]
    unnamed x28 -> x15, local copies, waits for them, and re-layouts: 1.88 us -> 10.5 us
    ppermute x0 -> x1, starting transfers between devices: none -> 3.65 us  [per_device(): other = lax.ppermute(send, 'top', [(0, 1), (1, 0)])]
  transfers between devices with their start and end apart: 1 -> 2, of which waited for: 0 -> 2; matrix products, arithmetic and copies ran while one was open for 16% -> 3% of each run, Pallas kernels for 0% -> 8%
where the time goes in v1:
time: 109 us; the launch traced here: 108 us
  Pallas kernels  61.9 us (57%)
  starting transfers between devices  20 us (18%)
  local copies, waits for them, and re-layouts  12.5 us (11%)
  waiting for transfers between devices  12.5 us (11%)
  other arithmetic  1.53 us (1%)
    pallas_call x1, Pallas kernels, per_device(): pl.pallas_call(functools.partial(main_kernel, order_terms), out_shape=(ha...  51.2 us
    all_to_all x1, starting transfers between devices, per_device(): lax.all_to_all(outgoing, 'leaf', split_axis=0, concat_axis=0, tiled=True)  16.3 us
    all_to_all x1, waiting for transfers between devices, per_device(): lax.all_to_all(outgoing, 'leaf', split_axis=0, concat_axis=0, tiled=True)  11.6 us
    unnamed x15, local copies, waits for them, and re-layouts  10.5 us
    pallas_call x1, Pallas kernels, arrange_classes(): pl.pallas_call(functools.partial(arrange_kernel, class_count), grid=(step...  8.67 us
    ppermute x1, starting transfers between devices, per_device(): other = lax.ppermute(send, 'top', [(0, 1), (1, 0)])  3.65 us
  transfers between devices with their start and end apart: 2, of which 2 were waited for; matrix products, arithmetic and copies ran while one was open for 3% of the time, Pallas kernels for 8%

profile of v1, /device:TPU:1, one launch (start us, length us, event | category | flops | bytes accessed | tf_op | source)
XLA Modules:
  0.0 108.5 jit_solution(353586483186018415)
XLA Ops:
  0.0 0.0 copy-start.3
  0.0 0.9 copy-done.3
  0.9 0.0 copy-start.4
  0.9 0.8 copy-done.4
  1.7 0.0 copy-start.5
  1.7 0.7 copy-done.5
  2.4 2.1 %shard_map.73 = bf16[128,32,128]{2,1,0:T(8,128)(2,1)} custom-call(bf16[121,128]{1,0:T(8,128)(2,1)S(1)} %copy-done.4, s32[16,128]{1,0:T(8,128)S(1)} %bitcast.17, bf16[968,121]{1,0:T(8,128)(2,1)S(1)} %bitcast.16), custom_call_target="tpu_custom_call" | custom-call | tf_op jit(solution)/shard_map/pallas_call | solution.py:297
  4.5 16.3 %all-to-all-start = ((bf16[128,32,128]{2,1,0:T(8,128)(2,1)}), bf16[128,32,128]{2,1,0:T(8,128)(2,1)S(1)}, u32[]{:S(2)}, u32[]{:S(2)}) async-start(bf16[128,32,128]{2,1,0:T(8,128)(2,1)} %shard_map.73), calls=%async_computation | async-start | bytes 2097152 | tf_op jit(solution)/shard_map/all_to_all | solution.py:308
  20.8 0.8 pad.13.local_cells
  21.6 0.9 fusion.5
  22.5 0.1 copy.13
  22.6 0.1 reshape.13.coarse_pos
  22.7 1.0 reshape.16
  23.7 0.2 copy.14
  23.9 0.1 pad.14.clone
  24.0 0.0 copy-start.2
  24.0 0.0 copy-start.1
  24.0 3.8 %copy-done.1 = bf16[121,38236]{0,1:T(8,128)(2,1)S(1)} copy-done((bf16[121,38236]{0,1:T(8,128)(2,1)S(1)}, bf16[121,38236]{0,1:T(8,128)(2,1)}, u32[]{:S(2)}) %copy-start.1) | copy-done | bytes 9253136
  27.8 8.7 %shard_map.74.operators = bf16[128,40960]{1,0:T(8,128)(2,1)} custom-call(bf16[38236,121]{1,0:T(8,128)(2,1)S(1)} %bitcast.14), custom_call_target="tpu_custom_call" | custom-call | bytes 41943040 | tf_op jit(solution)/shard_map/pallas_call | solution.py:242
  36.5 11.6 %all-to-all-done.arrived = bf16[128,32,128]{2,1,0:T(8,128)(2,1)S(1)} async-done(((bf16[128,32,128]{2,1,0:T(8,128)(2,1)}), bf16[128,32,128]{2,1,0:T(8,128)(2,1)S(1)}, u32[]{:S(2)}, u32[]{:S(2)}) %all-to-all-start) | async-done | bytes 1048608 | tf_op jit(solution)/shard_map/all_to_all | solution.py:308
  48.1 0.0 copy-done.2
  48.1 0.0 copy-start
  48.1 4.0 %copy-done = bf16[128,40960]{1,0:T(8,128)(2,1)S(1)} copy-done((bf16[128,40960]{1,0:T(8,128)(2,1)S(1)}, bf16[128,40960]{1,0:T(8,128)(2,1)}, u32[]{:S(2)}) %copy-start) | copy-done | bytes 10485784
  52.1 51.2 %shard_map.75 = (f32[128,128]{1,0:T(8,128)S(1)}, f32[128,128]{1,0:T(8,128)S(1)}) custom-call(s32[1]{0:T(128)} %bitcast.core_ref, s32[10240]{0:T(1024)S(1)} %reshape.13.coarse_pos, bf16[128,32,128]{2,1,0:T(8,128)(2,1)S(1)} %all-to-all-done.arrived, bf16[128,128]{1,0:T(8,128)(2,1)S(1)} %pad.13.local_cells, s32[316,256]{1,0:T(8,128)S(1)} %copy-done.2, ...), custom_call_target="tpu_custom_call" | custom-call | tf_op jit(solution)/shard_map/pallas_call | solution.py:325
  103.3 3.6 %collective-permute-start = (f32[128,128]{1,0:T(8,128)S(1)}, f32[128,128]{1,0:T(8,128)S(1)}, u32[]{:S(2)}, u32[]{:S(2)}) collective-permute-start(f32[128,128]{1,0:T(8,128)S(1)} %get-tuple-element.8), channel_id=1, source_target_pairs={{0,1},{1,0},{2,3},{3,2},{4,5},{5,4},{6,7},{7,6},{8,9},{9,8},{10,11... | collective-permute-start | bytes 196616 | tf_op jit(solution)/shard_map/ppermute | solution.py:340
  106.9 0.9 collective-permute-done
  107.8 0.6 slice_add_fusion
  (2 shorter events, 0.1 us)
Async XLA Ops:
  0.0 0.9 copy-start.3
  0.9 0.8 copy-start.4
  1.7 0.7 copy-start.5
  4.5 43.6 %all-to-all-start = ((bf16[128,32,128]{2,1,0:T(8,128)(2,1)}), bf16[128,32,128]{2,1,0:T(8,128)(2,1)S(1)}, u32[]{:S(2)}, u32[]{:S(2)}) async-start(bf16[128,32,128]{2,1,0:T(8,128)(2,1)} %shard_map.73), calls=%async_computation | async-start | bytes 2097152 | tf_op jit(solution)/shard_map/all_to_all | solution.py:308
  24.0 24.2 %copy-start.2 = (s32[316,256]{1,0:T(8,128)S(1)}, s32[316,256]{1,0:T(8,128)}, u32[]{:S(2)}) copy-start(s32[316,256]{1,0:T(8,128)} %pairs.1) | copy-start | bytes 970756
  24.0 3.8 %copy-start.1 = (bf16[121,38236]{0,1:T(8,128)(2,1)S(1)}, bf16[121,38236]{0,1:T(8,128)(2,1)}, u32[]{:S(2)}) copy-start(bf16[121,38236]{0,1:T(8,128)(2,1)} %param.9) | copy-start | bytes 27759340
  48.1 4.0 %copy-start = (bf16[128,40960]{1,0:T(8,128)(2,1)S(1)}, bf16[128,40960]{1,0:T(8,128)(2,1)}, u32[]{:S(2)}) copy-start(bf16[128,40960]{1,0:T(8,128)(2,1)} %shard_map.74.operators) | copy-start | bytes 31457284
  103.3 4.5 %collective-permute-start = (f32[128,128]{1,0:T(8,128)S(1)}, f32[128,128]{1,0:T(8,128)S(1)}, u32[]{:S(2)}, u32[]{:S(2)}) collective-permute-start(f32[128,128]{1,0:T(8,128)S(1)} %get-tuple-element.8), channel_id=1, source_target_pairs={{0,1},{1,0},{2,3},{3,2},{4,5},{5,4},{6,7},{7,6},{8,9},{9,8},{10,11... | collective-permute-start | bytes 196616 | tf_op jit(solution)/shard_map/ppermute | solution.py:340

commit v2 on v1

--- a/solution.py
+++ b/solution.py
@@ -15,6 +15,7 @@
 GROUP = 8
 TILE = 512
 HALF = TILE // 2
+BY_PRODUCT = (0, 3, 6)
 BLOCK = 128
 
 
@@ -35,17 +36,23 @@
     arrived,
     local_cells,
     pairs,
-    operators,
+    stored_operators,
     downward,
     keep,
     send,
+    operators,
+    arrival,
     places,
     tables,
+    columns,
     coarse_rows,
     picked,
+    cells,
     near_sum,
     coarse_sum,
 ):
+    fetch = pltpu.make_async_copy(stored_operators, operators, arrival)
+    fetch.start()
     core = core_ref[0]
     peers, rows_each, width = arrived.shape
     slots = rows_each // 2
@@ -100,7 +107,7 @@
         return jnp.concatenate(parts, axis=1)
 
     whole = class_count // 8
-    lax.fori_loop(0, whole, place, 0)
+    lax.fori_loop(0, whole, place, 0, unroll=4)
     tail = class_count - whole * 8
     if tail:
         rest = pairs[whole * 8 : class_count, :]
@@ -113,13 +120,15 @@
             one_hot = (
                 lax.broadcasted_iota(I32, (peers, slot_count), 0) + base == dest
             ).astype(F32).astype(BF)
-            cells = dot(one_hot, received).T.astype(BF)
+            packed = dot(one_hot, received).T.astype(BF)
             half, at = divmod(part * peers, HALF)
-            tables[tile, half * width : (half + 1) * width, at : at + peers] = cells
+            tables[tile, half * width : (half + 1) * width, at : at + peers] = packed
+            columns[tile, part] = packed.astype(F32)
         return 0
 
     lax.fori_loop(0, tile_count, pack, 0)
     tables[0, :width, :local_count] = local_cells[...]
+    columns[0, 0] = local_cells[...].astype(F32)
 
     coarse_rows[:slot_count, :] = arrived[:, slots:, :].reshape(slot_count, width).astype(F32)
     coarse_rows[slot_count:, :] = jnp.zeros((8, width), F32)
@@ -135,49 +144,88 @@
         both = dot(table, one_hot)
         return jnp.where(position >= HALF, both[width:], both[:width]).astype(BF)
 
-    def near_step(table, group, base):
-        position = places[pl.ds(pl.multiple_of(group * GROUP, GROUP), GROUP), :] - base
-        total = near_sum[...]
-        for pair in range(GROUP // 2):
-            cells = jnp.concatenate(
-                [gather(table, position[2 * pair + j : 2 * pair + j + 1]) for j in range(2)], axis=0
-            )
-            total = total + dot(operator_pair(group, pair), cells)
-        near_sum[...] = total
+    def lane_gather(tile, position):
+        blocks = []
+        for half in range(targets // width):
+            at = position[:, half * width : (half + 1) * width]
+            lane_at = jnp.broadcast_to(at & (width - 1), (8, width))
+            block = jnp.broadcast_to(at // width, (8, width))
+            block = jnp.where(jnp.broadcast_to(at, (8, width)) < 0, -1, block)
+            lines = []
+            for line in range(0, width, 8):
+                found = jnp.zeros((8, width), F32)
+                for part in range(TILE // width):
+                    picked_cells = jnp.take_along_axis(
+                        columns[tile, part, line : line + 8, :], lane_at, axis=1
+                    )
+                    found = jnp.where(block == part, picked_cells, found)
+                lines.append(found)
+            blocks.append(jnp.concatenate(lines, axis=0))
+        return jnp.concatenate(blocks, axis=1).astype(BF)
 
     def operator_pair(group, pair):
         start = pl.multiple_of((group * GROUP + 2 * pair) * width, 2 * width)
         return operators[:, pl.ds(start, 2 * width)]
 
-    def first_tile(group, _):
+    def near_step(table, tile, group, base, gather_now=True):
+        if gather_now:
+            position = places[pl.ds(pl.multiple_of(group * GROUP, GROUP), GROUP), :] - base
+        total = near_sum[...]
+        for pair in range(GROUP // 2):
+            here = slice(2 * pair * width, 2 * (pair + 1) * width)
+            ready = jnp.maximum(group - 1, 0)
+            total = total + dot(operator_pair(ready, pair), cells[here, :])
+            if gather_now:
+                for c in (2 * pair, 2 * pair + 1):
+                    row = position[c : c + 1]
+                    cells[c * width : (c + 1) * width, :] = (
+                        gather(table, row) if c in BY_PRODUCT else lane_gather(tile, row)
+                    )
+        near_sum[...] = total
+
+    def coarse_step(group, gather_now=True):
+        total = coarse_sum[...]
+        ready = jnp.maximum(group - 1, 0)
         base = group * (GROUP * coarse_targets)
-        for row in range(GROUP * coarse_targets):
-            picked[pl.ds(row, 1), :] = coarse_rows[pl.ds(coarse_pos[base + row], 1), :]
-        near_step(tables[0], group, 0)
-        total = coarse_sum[...]
         for pair in range(GROUP // 2):
             at = 2 * pair * coarse_targets
-            cells = jnp.concatenate(
+            both = jnp.concatenate(
                 [
                     picked[at + j * coarse_targets : at + (j + 1) * coarse_targets, :].astype(BF)
                     for j in range(2)
                 ],
                 axis=1,
             )
-            total = total + nt_dot(operator_pair(group, pair), cells)
+            total = total + nt_dot(operator_pair(ready, pair), both)
+            if gather_now:
+                for row in range(at, at + 2 * coarse_targets):
+                    picked[pl.ds(row, 1), :] = coarse_rows[pl.ds(coarse_pos[base + row], 1), :]
         coarse_sum[...] = total
-        return 0
-
+
+    picked[...] = jnp.zeros_like(picked)
+    cells[...] = jnp.zeros_like(cells)
+
+    def first_tile(group, _):
+        near_step(tables[0], 0, group, 0)
+        coarse_step(group)
+        return 0
+
+    fetch.wait()
     lax.fori_loop(0, groups, first_tile, 0)
+    coarse_step(groups, False)
+    near_step(None, 0, groups, 0, False)
 
     def more_tiles(tile, _):
         table = tables[tile]
+        cells[...] = jnp.zeros_like(cells)
 
         def step(group, _):
-            near_step(table, group, tile * TILE)
+            near_step(table, tile, group, tile * TILE)
             return 0
 
-        return lax.fori_loop(0, groups, step, 0)
+        lax.fori_loop(0, groups, step, 0)
+        near_step(None, tile, groups, 0, False)
+        return 0
 
     lax.fori_loop(1, tile_count, more_tiles, 0)
 
@@ -325,17 +373,21 @@
     keep, send = pl.pallas_call(
         functools.partial(main_kernel, order_terms),
         out_shape=(half_shape, half_shape),
-        in_specs=[smem, smem] + [vmem] * 5,
+        in_specs=[smem, smem] + [vmem] * 3 + [pl.BlockSpec(memory_space=pl.ANY), vmem],
         out_specs=(vmem, vmem),
         scratch_shapes=[
+            pltpu.VMEM(operators.shape, BF),
+            pltpu.SemaphoreType.DMA,
             pltpu.VMEM((padded_classes, targets), I32),
             pltpu.VMEM((most_tiles, 2 * WIDTH, HALF), BF),
+            pltpu.VMEM((most_tiles, TILE // WIDTH, WIDTH, WIDTH), F32),
             pltpu.VMEM((zero_row + 8, WIDTH), F32),
             pltpu.VMEM((GROUP * coarse_targets, WIDTH), F32),
+            pltpu.VMEM((GROUP * WIDTH, targets), BF),
             pltpu.VMEM((WIDTH, targets), F32),
             pltpu.VMEM((WIDTH, coarse_targets), F32),
         ],
-        compiler_params=pltpu.CompilerParams(vmem_limit_bytes=40 << 20),
+        compiler_params=pltpu.CompilerParams(vmem_limit_bytes=60 << 20),
     )(core.reshape(1), coarse_pos, arrived, local_cells, leaf_pairs, operators, downward)
     other = lax.ppermute(send, "top", [(0, 1), (1, 0)])
     return (keep + other)[:order_terms]

time: 109 us -> 86.5 us (0.79)
  Pallas kernels: 61.9 us -> 41.2 us
  waiting for transfers between devices: 12.5 us -> 10.9 us
  local copies, waits for them, and re-layouts: 12.5 us -> 11.3 us
    pallas_call x1, Pallas kernels: 51.2 us -> 30.5 us  [per_device(): pl.pallas_call(functools.partial(main_kernel, order_terms), out_shape=(ha...]
    unnamed x15 -> x13, local copies, waits for them, and re-layouts: 10.5 us -> 8.18 us
    all_to_all x1, waiting for transfers between devices: 11.6 us -> 9.77 us  [per_device(): lax.all_to_all(outgoing, 'leaf', split_axis=0, concat_axis=0, tiled=True)]
  transfers between devices with their start and end apart: 2 -> 2, of which waited for: 2 -> 2; matrix products, arithmetic and copies ran while one was open for 3% -> 6% of each run, Pallas kernels for 8% -> 10%
where the time goes in v2:
time: 86.5 us; the launch traced here: 85.9 us
  Pallas kernels  41.2 us (48%)
  starting transfers between devices  20 us (23%)
  local copies, waits for them, and re-layouts  11.3 us (13%)
  waiting for transfers between devices  10.9 us (13%)
  other arithmetic  2.37 us (3%)
    pallas_call x1, Pallas kernels, per_device(): pl.pallas_call(functools.partial(main_kernel, order_terms), out_shape=(ha...  30.5 us
    all_to_all x1, starting transfers between devices, per_device(): lax.all_to_all(outgoing, 'leaf', split_axis=0, concat_axis=0, tiled=True)  16.3 us
    all_to_all x1, waiting for transfers between devices, per_device(): lax.all_to_all(outgoing, 'leaf', split_axis=0, concat_axis=0, tiled=True)  9.77 us
    pallas_call x1, Pallas kernels, arrange_classes(): pl.pallas_call(functools.partial(arrange_kernel, class_count), grid=(step...  8.64 us
    unnamed x13, local copies, waits for them, and re-layouts  8.18 us
    ppermute x1, starting transfers between devices, per_device(): other = lax.ppermute(send, 'top', [(0, 1), (1, 0)])  3.68 us
    pallas_call x1, Pallas kernels, per_device(): pl.pallas_call(outgoing_kernel, out_shape=jax.ShapeDtypeStruct((peers, sl...  2.06 us
  transfers between devices with their start and end apart: 2, of which 2 were waited for; matrix products, arithmetic and copies ran while one was open for 6% of the time, Pallas kernels for 10%

profile of v2, /device:TPU:1, one launch (start us, length us, event | category | flops | bytes accessed | tf_op | source)
XLA Modules:
  0.0 85.9 jit_solution(7370476069665358749)
XLA Ops:
  0.0 0.0 copy-start.1
  0.0 0.9 %copy-done.1 = bf16[121,968]{0,1:T(8,128)(2,1)S(1)} copy-done((bf16[121,968]{0,1:T(8,128)(2,1)S(1)}, bf16[121,968]{0,1:T(8,128)(2,1)}, u32[]{:S(2)}) %copy-start.1) | copy-done | bytes 234280
  0.9 0.0 copy-start.2
  0.9 0.8 copy-done.2
  1.7 0.0 copy-start.3
  1.7 0.7 copy-done.3
  2.4 2.1 %shard_map.73 = bf16[128,32,128]{2,1,0:T(8,128)(2,1)} custom-call(bf16[121,128]{1,0:T(8,128)(2,1)S(1)} %copy-done.2, s32[16,128]{1,0:T(8,128)S(1)} %bitcast.16, bf16[968,121]{1,0:T(8,128)(2,1)S(1)} %bitcast.15), custom_call_target="tpu_custom_call" | custom-call | tf_op jit(solution)/shard_map/pallas_call | solution.py:345
  4.5 16.3 %all-to-all-start = ((bf16[128,32,128]{2,1,0:T(8,128)(2,1)}), bf16[128,32,128]{2,1,0:T(8,128)(2,1)S(1)}, u32[]{:S(2)}, u32[]{:S(2)}) async-start(bf16[128,32,128]{2,1,0:T(8,128)(2,1)} %shard_map.73), calls=%async_computation | async-start | bytes 2097152 | tf_op jit(solution)/shard_map/all_to_all | solution.py:356
  20.8 1.4 %pad.13.local_cells = bf16[128,128]{1,0:T(8,128)(2,1)} pad(bf16[121,128]{1,0:T(8,128)(2,1)} %cells.1, bf16[]{:T(256)} %constant.60.clone.1), padding=0_7x0_0 | pad | bytes 63746 | tf_op jit(solution)/shard_map/jit(_pad)/pad | solution.py:358
  22.2 0.9 %fusion.5 = s32[316,32]{0,1:T(8,128)S(1)} fusion(s32[316,32]{0,1:T(8,128)} %param.13, s32[]{:T(128)} %axis_index.12), kind=kLoop, calls=%fused_computation.18 | loop fusion | flops 465152 | bytes 80900 | tf_op jit(solution)/shard_map/jit(_where)/select_n | solution.py:366
  23.1 0.1 copy.13
  23.2 0.7 reshape.13.coarse_pos
  23.9 1.0 %reshape.16 = bf16[121,8,121]{0,2,1:T(8,128)(2,1)S(1)} reshape(bf16[121,968]{0,1:T(8,128)(2,1)} %param.10) | data formatting | bytes 468512 | tf_op jit(solution)/shard_map/reshape | solution.py:256
  24.9 0.2 copy.14
  25.1 0.1 pad.14.clone
  25.2 0.8 copy.18
  25.9 0.0 copy-start
  25.9 3.8 %copy-done = bf16[121,38236]{0,1:T(8,128)(2,1)S(1)} copy-done((bf16[121,38236]{0,1:T(8,128)(2,1)S(1)}, bf16[121,38236]{0,1:T(8,128)(2,1)}, u32[]{:S(2)}) %copy-start) | copy-done | bytes 9253136
  29.7 8.6 %shard_map.74.stored_operators = bf16[128,40960]{1,0:T(8,128)(2,1)} custom-call(bf16[38236,121]{1,0:T(8,128)(2,1)S(1)} %bitcast.14), custom_call_target="tpu_custom_call" | custom-call | bytes 41943040 | tf_op jit(solution)/shard_map/pallas_call | solution.py:290
  38.3 9.8 %all-to-all-done.arrived = bf16[128,32,128]{2,1,0:T(8,128)(2,1)S(1)} async-done(((bf16[128,32,128]{2,1,0:T(8,128)(2,1)}), bf16[128,32,128]{2,1,0:T(8,128)(2,1)S(1)}, u32[]{:S(2)}, u32[]{:S(2)}) %all-to-all-start) | async-done | bytes 1048608 | tf_op jit(solution)/shard_map/all_to_all | solution.py:356
  48.1 0.0 copy-start.4
  48.1 1.0 %copy-done.4 = bf16[128,32,128]{2,1,0:T(8,128)(2,1)} copy-done((bf16[128,32,128]{2,1,0:T(8,128)(2,1)}, bf16[128,32,128]{2,1,0:T(8,128)(2,1)S(1)}, u32[]{:S(2)}) %copy-start.4) | copy-done | bytes 1048600
  49.1 30.5 %shard_map.75 = (f32[128,128]{1,0:T(8,128)}, f32[128,128]{1,0:T(8,128)}) custom-call(s32[1]{0:T(128)} %bitcast.core_ref, s32[10240]{0:T(1024)} %reshape.13.coarse_pos, bf16[128,32,128]{2,1,0:T(8,128)(2,1)} %copy-done.4, bf16[128,128]{1,0:T(8,128)(2,1)} %pad.13.local_cells, s32[316,256]{1,0:T(8,128)} %pairs.1, bf16[128,40960]{1,0:T(8,128)(2,1)} %shard_map.74.stored_operators, ...), custom_call_target="tpu_custom_call" | custom-call | tf_op jit(solution)/shard_map/pallas_call | solution.py:373
  79.6 3.7 %collective-permute-start = (f32[128,128]{1,0:T(8,128)}, f32[128,128]{1,0:T(8,128)S(1)}, u32[]{:S(2)}, u32[]{:S(2)}) collective-permute-start(f32[128,128]{1,0:T(8,128)} %get-tuple-element.8), channel_id=1, source_target_pairs={{0,1},{1,0},{2,3},{3,2},{4,5},{5,4},{6,7},{7,6},{8,9},{9,8},{10,11... | collective-permute-start | bytes 196616 | tf_op jit(solution)/shard_map/ppermute | solution.py:392
  83.3 1.1 %collective-permute-done = f32[128,128]{1,0:T(8,128)S(1)} collective-permute-done((f32[128,128]{1,0:T(8,128)}, f32[128,128]{1,0:T(8,128)S(1)}, u32[]{:S(2)}, u32[]{:S(2)}) %collective-permute-start) | collective-permute-done | bytes 65568 | tf_op jit(solution)/shard_map/ppermute | solution.py:392
  84.4 1.5 %slice_add_fusion = f32[121,128]{1,0:T(8,128)} fusion(f32[128,128]{1,0:T(8,128)S(1)} %collective-permute-done, f32[128,128]{1,0:T(8,128)} %get-tuple-element.7), kind=kLoop, calls=%fused_computation.12 | loop fusion | flops 15488 | bytes 185856 | tf_op jit(solution)/shard_map/add | solution.py:393
  (1 shorter events, 0.0 us)
Async XLA Ops:
  0.0 0.9 %copy-start.1 = (bf16[121,968]{0,1:T(8,128)(2,1)S(1)}, bf16[121,968]{0,1:T(8,128)(2,1)}, u32[]{:S(2)}) copy-start(bf16[121,968]{0,1:T(8,128)(2,1)} %param.8) | copy-start | bytes 702772
  0.9 0.8 copy-start.2
  1.7 0.7 copy-start.3
  4.5 43.6 %all-to-all-start = ((bf16[128,32,128]{2,1,0:T(8,128)(2,1)}), bf16[128,32,128]{2,1,0:T(8,128)(2,1)S(1)}, u32[]{:S(2)}, u32[]{:S(2)}) async-start(bf16[128,32,128]{2,1,0:T(8,128)(2,1)} %shard_map.73), calls=%async_computation | async-start | bytes 2097152 | tf_op jit(solution)/shard_map/all_to_all | solution.py:356
  25.9 3.8 %copy-start = (bf16[121,38236]{0,1:T(8,128)(2,1)S(1)}, bf16[121,38236]{0,1:T(8,128)(2,1)}, u32[]{:S(2)}) copy-start(bf16[121,38236]{0,1:T(8,128)(2,1)} %param.9) | copy-start | bytes 27759340
  48.1 1.0 %copy-start.4 = (bf16[128,32,128]{2,1,0:T(8,128)(2,1)}, bf16[128,32,128]{2,1,0:T(8,128)(2,1)S(1)}, u32[]{:S(2)}) copy-start(bf16[128,32,128]{2,1,0:T(8,128)(2,1)S(1)} %all-to-all-done.arrived) | copy-start | bytes 3145732
  79.6 4.8 %collective-permute-start = (f32[128,128]{1,0:T(8,128)}, f32[128,128]{1,0:T(8,128)S(1)}, u32[]{:S(2)}, u32[]{:S(2)}) collective-permute-start(f32[128,128]{1,0:T(8,128)} %get-tuple-element.8), channel_id=1, source_target_pairs={{0,1},{1,0},{2,3},{3,2},{4,5},{5,4},{6,7},{7,6},{8,9},{9,8},{10,11... | collective-permute-start | bytes 196616 | tf_op jit(solution)/shard_map/ppermute | solution.py:392

commit v3 on v2

--- a/solution.py
+++ b/solution.py
@@ -12,10 +12,12 @@
 I32 = jnp.int32
 
 WIDTH = 128
-GROUP = 8
-TILE = 512
-HALF = TILE // 2
-BY_PRODUCT = (0, 3, 6)
+GROUP = 16
+TILE = 384
+HALF = 256
+FETCHES = 4
+SPAN = 8
+BY_PRODUCT = (0, 3, 6, 8, 11, 14)
 BLOCK = 128
 
 
@@ -34,14 +36,14 @@
     core_ref,
     coarse_pos,
     arrived,
-    local_cells,
     pairs,
+    local_sum,
     stored_operators,
     downward,
     keep,
     send,
     operators,
-    arrival,
+    arrivals,
     places,
     tables,
     columns,
@@ -51,8 +53,16 @@
     near_sum,
     coarse_sum,
 ):
-    fetch = pltpu.make_async_copy(stored_operators, operators, arrival)
-    fetch.start()
+    piece = operators.shape[1] // FETCHES
+
+    def fetch(index):
+        span = pl.ds(pl.multiple_of(index * piece, WIDTH), piece)
+        return pltpu.make_async_copy(
+            stored_operators.at[:, span], operators.at[:, span], arrivals.at[index]
+        )
+
+    for index in range(FETCHES):
+        fetch(index).start()
     core = core_ref[0]
     peers, rows_each, width = arrived.shape
     slots = rows_each // 2
@@ -60,7 +70,7 @@
     class_count, targets = pairs.shape
     groups = places.shape[0] // GROUP
     coarse_targets = coarse_sum.shape[1]
-    local_count = local_cells.shape[1]
+    local_count = targets // 2
 
     received = arrived[:, :slots, :].reshape(slot_count, width)
     flag_pick = (lax.broadcasted_iota(I32, (16, width), 1) == flag_lane).astype(F32).astype(BF)
@@ -73,9 +83,9 @@
     before = (
         lax.broadcasted_iota(I32, (peers, peers), 0) < lax.broadcasted_iota(I32, (peers, peers), 1)
     )
-    first = dot(counts.astype(BF), before.astype(F32).astype(BF))[:8].astype(I32) + local_count
+    first = dot(counts.astype(BF), before.astype(F32).astype(BF))[:8].astype(I32)
     used = jnp.sum(counts[0:1, :]).astype(I32)
-    tile_count = (local_count + used + TILE - 1) // TILE
+    tile_count = (used + TILE - 1) // TILE
 
     lane = lax.broadcasted_iota(I32, (8, peers), 1)
     dest_parts = []
@@ -86,33 +96,32 @@
         dest_parts.append(jnp.where(live, at, -1))
     dest = jnp.concatenate(dest_parts, axis=1)[0:1]
 
-    def place(row, _):
-        start = pl.multiple_of(row * 8, 8)
-        inside = pairs[pl.ds(start, 8), :]
-        places[pl.ds(start, 8), :] = place_rows(inside)
-        return 0
-
     def place_rows(column):
+        lines = column.shape[0]
+        from_peer = jnp.broadcast_to(first[0:1], (lines, peers))
         parts = []
         for half in range(targets // peers):
             col = column[:, half * peers : (half + 1) * peers]
             slot = col - 2 * local_count - core * slot_count
             mine = (slot >= 0) & (slot < slot_count)
             safe = jnp.where(mine, slot, 0)
-            far = jnp.take_along_axis(first, safe // slots, axis=1) + safe % slots
-            near = col - core * local_count
-            parts.append(
-                jnp.where(mine, far, jnp.where((near >= 0) & (near < local_count), near, -1))
-            )
+            far = jnp.take_along_axis(from_peer, safe // slots, axis=1) + safe % slots
+            parts.append(jnp.where(mine, far, -1))
         return jnp.concatenate(parts, axis=1)
 
-    whole = class_count // 8
-    lax.fori_loop(0, whole, place, 0, unroll=4)
-    tail = class_count - whole * 8
-    if tail:
-        rest = pairs[whole * 8 : class_count, :]
-        rest = jnp.concatenate([rest, jnp.full((8 - tail, targets), 1 << 20, I32)], axis=0)
-        places[whole * 8 : whole * 8 + 8, :] = place_rows(rest)
+    lines = 32
+
+    def place(block, _):
+        start = pl.multiple_of(block * lines, lines)
+        places[pl.ds(start, lines), :] = place_rows(pairs[pl.ds(start, lines), :])
+        return 0
+
+    whole = class_count // lines * lines
+    lax.fori_loop(0, whole // lines, place, 0)
+    for start in range(whole, class_count, 8):
+        count = min(8, class_count - start)
+        places[start : start + count, :] = place_rows(pairs[start : start + count, :])
+    places[class_count:, :] = jnp.full((places.shape[0] - class_count, targets), -1, I32)
 
     def pack(tile, _):
         for part in range(TILE // peers):
@@ -126,14 +135,13 @@
             columns[tile, part] = packed.astype(F32)
         return 0
 
-    lax.fori_loop(0, tile_count, pack, 0)
-    tables[0, :width, :local_count] = local_cells[...]
-    columns[0, 0] = local_cells[...].astype(F32)
+    tables[...] = jnp.zeros_like(tables)
+    lax.fori_loop(0, jnp.maximum(tile_count, 1), pack, 0)
 
     coarse_rows[:slot_count, :] = arrived[:, slots:, :].reshape(slot_count, width).astype(F32)
     coarse_rows[slot_count:, :] = jnp.zeros((8, width), F32)
 
-    near_sum[...] = jnp.zeros_like(near_sum)
+    near_sum[...] = local_sum[...]
     coarse_sum[...] = jnp.zeros_like(coarse_sum)
     row_index = lax.broadcasted_iota(I32, (HALF, targets), 0)
 
@@ -167,14 +175,19 @@
         start = pl.multiple_of((group * GROUP + 2 * pair) * width, 2 * width)
         return operators[:, pl.ds(start, 2 * width)]
 
+    def operator_span(group, pair):
+        start = pl.multiple_of((group * GROUP + 2 * pair) * width, 2 * width)
+        return operators[:, pl.ds(start, 2 * SPAN * width)]
+
     def near_step(table, tile, group, base, gather_now=True):
         if gather_now:
             position = places[pl.ds(pl.multiple_of(group * GROUP, GROUP), GROUP), :] - base
         total = near_sum[...]
         for pair in range(GROUP // 2):
-            here = slice(2 * pair * width, 2 * (pair + 1) * width)
+            here = slice(2 * pair * width, 2 * (pair + SPAN) * width)
             ready = jnp.maximum(group - 1, 0)
-            total = total + dot(operator_pair(ready, pair), cells[here, :])
+            if pair % SPAN == 0:
+                total = total + dot(operator_span(ready, pair), cells[here, :])
             if gather_now:
                 for c in (2 * pair, 2 * pair + 1):
                     row = position[c : c + 1]
@@ -210,8 +223,13 @@
         coarse_step(group)
         return 0
 
-    fetch.wait()
-    lax.fori_loop(0, groups, first_tile, 0)
+    steps = groups // FETCHES
+
+    def fetched(index, _):
+        fetch(index).wait()
+        return lax.fori_loop(index * steps, (index + 1) * steps, first_tile, 0)
+
+    lax.fori_loop(0, FETCHES, fetched, 0)
     coarse_step(groups, False)
     near_step(None, 0, groups, 0, False)
 
@@ -251,6 +269,45 @@
     send[...] = jnp.where(core == 0, right, left)
 
 
+def local_kernel(core_ref, local_cells, pairs, operators, local_sum, places, columns, cells):
+    width, local_count = local_cells.shape
+    class_count, targets = pairs.shape
+    groups = places.shape[0] // GROUP
+    first = core_ref[0] * local_count
+    places[:class_count, :] = pairs[...] - first
+    places[class_count:, :] = jnp.full((places.shape[0] - class_count, targets), -1, I32)
+    columns[...] = local_cells[...].astype(F32)
+    cells[...] = jnp.zeros_like(cells)
+    local_sum[...] = jnp.zeros_like(local_sum)
+
+    def translate(group):
+        start = pl.multiple_of(group * GROUP * width, GROUP * width)
+        local_sum[...] += dot(operators[:, pl.ds(start, GROUP * width)], cells[...])
+
+    def step(group, _):
+        translate(jnp.maximum(group - 1, 0))
+        position = places[pl.ds(pl.multiple_of(group * GROUP, GROUP), GROUP), :]
+        for c in range(GROUP):
+            for half in range(targets // width):
+                span = slice(half * width, (half + 1) * width)
+                at = jnp.broadcast_to(position[c : c + 1, span], (8, width))
+                live = (at >= 0) & (at < local_count)
+                lane_at = at & (local_count - 1)
+                lines = [
+                    jnp.where(
+                        live,
+                        jnp.take_along_axis(columns[line : line + 8, :], lane_at, axis=1),
+                        0.0,
+                    )
+                    for line in range(0, width, 8)
+                ]
+                cells[c * width : (c + 1) * width, span] = jnp.concatenate(lines, axis=0).astype(BF)
+        return 0
+
+    lax.fori_loop(0, groups, step, 0)
+    translate(groups - 1)
+
+
 def arrange(operators, order_terms):
     class_count = operators.shape[1] // order_terms
     arranged = operators.reshape(order_terms, class_count, order_terms).transpose(2, 1, 0)
@@ -261,40 +318,47 @@
 
 def arrange_kernel(class_count, source, arranged, rows):
     lines, order_terms = source.shape
-    step = pl.program_id(0)
-    rows[:, order_terms:] = jnp.zeros((lines + 8, WIDTH - order_terms), F32)
-    rows[lines:, :] = jnp.zeros((8, WIDTH), F32)
-
-    def widen(block, _):
-        start = pl.multiple_of(block * WIDTH, WIDTH)
-        rows[pl.ds(start, WIDTH), :order_terms] = source[pl.ds(start, WIDTH), :].astype(F32)
-        return 0
-
-    lax.fori_loop(0, lines // WIDTH, widen, 0, unroll=4)
-
-    def cut(index, _):
-        start = pl.multiple_of(index * WIDTH, WIDTH)
-        real = step * BLOCK + index < class_count
-        square = jnp.where(real, rows[pl.ds(index * order_terms, WIDTH), :], 0.0)
-        arranged[:, pl.ds(start, WIDTH)] = square.astype(BF)
-        return 0
-
-    lax.fori_loop(0, BLOCK, cut, 0, unroll=4)
+    whole = rows.shape[0] - 8
+    rows[:, order_terms:] = jnp.zeros((whole + 8, WIDTH - order_terms), F32)
+    rows[whole:, :] = jnp.zeros((8, WIDTH), F32)
+    for done in range(0, class_count, BLOCK):
+        here = min(BLOCK, class_count - done)
+        count = here * order_terms
+        start = done * order_terms
+
+        def widen(block, _):
+            at = pl.multiple_of(block * WIDTH, WIDTH)
+            rows[pl.ds(at, WIDTH), :order_terms] = source[pl.ds(start + at, WIDTH), :].astype(F32)
+            return 0
+
+        lax.fori_loop(0, count // WIDTH, widen, 0, unroll=4)
+        left = count % WIDTH
+        if left:
+            rows[count - left : count, :order_terms] = source[
+                start + count - left : start + count, :
+            ].astype(F32)
+
+        def cut(index, _):
+            at = pl.multiple_of((done + index) * WIDTH, WIDTH)
+            arranged[:, pl.ds(at, WIDTH)] = rows[pl.ds(index * order_terms, WIDTH), :].astype(BF)
+            return 0
+
+        lax.fori_loop(0, here, cut, 0, unroll=4)
+    spare = arranged.shape[1] - class_count * WIDTH
+    arranged[:, class_count * WIDTH :] = jnp.zeros((WIDTH, spare), BF)
 
 
 def arrange_classes(operators, order_terms):
     class_count = operators.shape[0] // order_terms
     padded_count = (class_count + GROUP - 1) // GROUP * GROUP
-    lines = BLOCK * order_terms
-    steps = (class_count + BLOCK - 1) // BLOCK
+    vmem = pl.BlockSpec(memory_space=pltpu.VMEM)
     return pl.pallas_call(
         functools.partial(arrange_kernel, class_count),
-        grid=(steps,),
         out_shape=jax.ShapeDtypeStruct((WIDTH, padded_count * WIDTH), BF),
-        in_specs=[pl.BlockSpec((lines, order_terms), lambda step: (step, 0))],
-        out_specs=pl.BlockSpec((WIDTH, BLOCK * WIDTH), lambda step: (0, step)),
-        scratch_shapes=[pltpu.VMEM((lines + 8, WIDTH), F32)],
-        compiler_params=pltpu.CompilerParams(vmem_limit_bytes=40 << 20),
+        in_specs=[vmem],
+        out_specs=vmem,
+        scratch_shapes=[pltpu.VMEM((BLOCK * order_terms + 8, WIDTH), F32)],
+        compiler_params=pltpu.CompilerParams(vmem_limit_bytes=32 << 20),
         cost_estimate=pl.CostEstimate(
             flops=0, bytes_accessed=40 * 1024 * 1024, transcendentals=0
         ),
@@ -345,20 +409,39 @@
     outgoing = pl.pallas_call(
         outgoing_kernel,
         out_shape=jax.ShapeDtypeStruct((peers, slots + coarse_count, WIDTH), BF),
-        in_specs=[vmem] * 3,
-        out_specs=vmem,
+        grid=(1,),
+        in_specs=[
+            pl.BlockSpec(shape, lambda step: (0, 0))
+            for shape in (leaf_multipoles.shape, (slots, peers), upward_ops.shape[::-1])
+        ],
+        out_specs=pl.BlockSpec((peers, slots + coarse_count, WIDTH), lambda step: (0, 0, 0)),
         scratch_shapes=[
             pltpu.VMEM((peers * slots, WIDTH), F32),
             pltpu.VMEM((8 * order_terms + 8, cell_count), F32),
         ],
-        compiler_params=pltpu.CompilerParams(vmem_limit_bytes=16 << 20),
+        compiler_params=pltpu.CompilerParams(vmem_limit_bytes=60 << 20),
     )(leaf_multipoles, send_lists[0].T, upward_ops.T)
     arrived = lax.all_to_all(outgoing, "leaf", split_axis=0, concat_axis=0, tiled=True)
 
     local_cells = jnp.pad(leaf_multipoles, ((0, WIDTH - order_terms), (0, 0)))
     operators = arrange_classes(transfer_ops.T, order_terms)
+    padded_classes = operators.shape[1] // WIDTH
+    local_sum = pl.pallas_call(
+        local_kernel,
+        out_shape=jax.ShapeDtypeStruct((WIDTH, targets), F32),
+        in_specs=[smem, vmem, vmem, vmem],
+        out_specs=vmem,
+        scratch_shapes=[
+            pltpu.VMEM((padded_classes, targets), I32),
+            pltpu.VMEM((WIDTH, cell_count), F32),
+            pltpu.VMEM((GROUP * WIDTH, targets), BF),
+        ],
+        compiler_params=pltpu.CompilerParams(vmem_limit_bytes=24 << 20),
+        cost_estimate=pl.CostEstimate(
+            flops=0, bytes_accessed=30 * 1024 * 1024, transcendentals=0
+        ),
+    )(core.reshape(1), local_cells, leaf_pairs, operators)
     downward = arrange(downward_ops, order_terms)
-    padded_classes = operators.shape[1] // WIDTH
     source_core = (top_pairs // coarse_count) % 2
     source_row = top_pairs // (2 * coarse_count) * coarse_count + top_pairs % coarse_count
     zero_row = peers * coarse_count
@@ -368,7 +451,7 @@
         coarse_pos, ((0, padded_classes - class_count), (0, 0)), constant_values=zero_row
     ).reshape(-1)
 
-    most_tiles = (cell_count + peers * slots + TILE - 1) // TILE
+    most_tiles = (peers * slots + TILE - 1) // TILE
     half_shape = jax.ShapeDtypeStruct((WIDTH, cell_count), F32)
     keep, send = pl.pallas_call(
         functools.partial(main_kernel, order_terms),
@@ -377,7 +460,7 @@
         out_specs=(vmem, vmem),
         scratch_shapes=[
             pltpu.VMEM(operators.shape, BF),
-            pltpu.SemaphoreType.DMA,
+            pltpu.SemaphoreType.DMA((FETCHES,)),
             pltpu.VMEM((padded_classes, targets), I32),
             pltpu.VMEM((most_tiles, 2 * WIDTH, HALF), BF),
             pltpu.VMEM((most_tiles, TILE // WIDTH, WIDTH, WIDTH), F32),
@@ -387,8 +470,8 @@
             pltpu.VMEM((WIDTH, targets), F32),
             pltpu.VMEM((WIDTH, coarse_targets), F32),
         ],
-        compiler_params=pltpu.CompilerParams(vmem_limit_bytes=60 << 20),
-    )(core.reshape(1), coarse_pos, arrived, local_cells, leaf_pairs, operators, downward)
+        compiler_params=pltpu.CompilerParams(vmem_limit_bytes=51 << 20),
+    )(core.reshape(1), coarse_pos, arrived, leaf_pairs, local_sum, operators, downward)
     other = lax.ppermute(send, "top", [(0, 1), (1, 0)])
     return (keep + other)[:order_terms]
 

time: 86.5 us -> 76.6 us (0.89)
  waiting for transfers between devices: 10.9 us -> 3.18 us
  local copies, waits for them, and re-layouts: 11.3 us -> 10 us
    all_to_all x1, waiting for transfers between devices: 9.77 us -> 2.28 us  [per_device(): lax.all_to_all(outgoing, 'leaf', split_axis=0, concat_axis=0, tiled=True)]
    pallas_call x1, Pallas kernels: 30.5 us -> 24.4 us  [per_device(): pl.pallas_call(functools.partial(main_kernel, order_terms), out_shape=(ha...]
    pallas_call x1 -> x2, Pallas kernels: 8.64 us -> 14 us  [the longest x1 9.72 us: per_device(): pl.pallas_call(local_kernel, out_shape=jax.ShapeDtypeStruct((WIDTH, targe...]
    pallas_call x1, Pallas kernels: 2.06 us -> 3.02 us  [per_device(): pl.pallas_call(outgoing_kernel, out_shape=jax.ShapeDtypeStruct((peers, sl...]
    unnamed x13 -> x9, local copies, waits for them, and re-layouts: 8.18 us -> 8.1 us
  transfers between devices with their start and end apart: 2 -> 2, of which waited for: 2 -> 2; matrix products, arithmetic and copies ran while one was open for 6% -> 4% of each run, Pallas kernels for 10% -> 18%
where the time goes in v3:
time: 76.6 us; the launch traced here: 76.2 us
  Pallas kernels  41.4 us (54%)
  starting transfers between devices  20 us (26%)
  local copies, waits for them, and re-layouts  10 us (13%)
  waiting for transfers between devices  3.18 us (4%)
  other arithmetic  1.53 us (2%)
    pallas_call x1, Pallas kernels, per_device(): pl.pallas_call(functools.partial(main_kernel, order_terms), out_shape=(ha...  24.4 us
    all_to_all x1, starting transfers between devices, per_device(): lax.all_to_all(outgoing, 'leaf', split_axis=0, concat_axis=0, tiled=True)  16.3 us
    pallas_call x1, Pallas kernels, per_device(): pl.pallas_call(local_kernel, out_shape=jax.ShapeDtypeStruct((WIDTH, targe...  9.72 us
    unnamed x9, local copies, waits for them, and re-layouts  8.1 us
    pallas_call x1, Pallas kernels, arrange_classes(): pl.pallas_call(functools.partial(arrange_kernel, class_count), out_shape=...  4.28 us
    ppermute x1, starting transfers between devices, per_device(): other = lax.ppermute(send, 'top', [(0, 1), (1, 0)])  3.65 us
    pallas_call x1, Pallas kernels, per_device(): pl.pallas_call(outgoing_kernel, out_shape=jax.ShapeDtypeStruct((peers, sl...  3.02 us
    all_to_all x1, waiting for transfers between devices, per_device(): lax.all_to_all(outgoing, 'leaf', split_axis=0, concat_axis=0, tiled=True)  2.28 us
  transfers between devices with their start and end apart: 2, of which 2 were waited for; matrix products, arithmetic and copies ran while one was open for 4% of the time, Pallas kernels for 18%

profile of v3, /device:TPU:1, one launch (start us, length us, event | category | flops | bytes accessed | tf_op | source)
XLA Modules:
  0.0 76.2 jit_solution(18038308656235791528)
XLA Ops:
  0.0 3.0 %shard_map.73 = bf16[128,32,128]{2,1,0:T(8,128)(2,1)} custom-call(bf16[121,128]{1,0:T(8,128)(2,1)} %cells.1, s32[16,128]{1,0:T(8,128)} %bitcast.19, bf16[968,121]{1,0:T(8,128)(2,1)} %bitcast.18), custom_call_target="tpu_custom_call" | custom-call | tf_op jit(solution)/shard_map/pallas_call | solution.py:409
  3.0 16.3 %all-to-all-start = ((bf16[128,32,128]{2,1,0:T(8,128)(2,1)}), bf16[128,32,128]{2,1,0:T(8,128)(2,1)S(1)}, u32[]{:S(2)}, u32[]{:S(2)}) async-start(bf16[128,32,128]{2,1,0:T(8,128)(2,1)} %shard_map.73), calls=%async_computation | async-start | bytes 2097152 | tf_op jit(solution)/shard_map/all_to_all | solution.py:424
  19.4 0.8 %pad.13.local_cells = bf16[128,128]{1,0:T(8,128)(2,1)S(1)} pad(bf16[121,128]{1,0:T(8,128)(2,1)} %cells.1, bf16[]{:T(256)} %constant.60.clone.1), padding=0_7x0_0 | pad | bytes 63746 | tf_op jit(solution)/shard_map/jit(_pad)/pad | solution.py:426
  20.1 0.9 %fusion.5 = s32[316,32]{0,1:T(8,128)S(1)} fusion(s32[316,32]{0,1:T(8,128)} %param.13, s32[]{:T(128)} %axis_index.12), kind=kLoop, calls=%fused_computation.18 | loop fusion | flops 465152 | bytes 80900 | tf_op jit(solution)/shard_map/jit(_where)/select_n | solution.py:449
  21.0 0.1 copy.13
  21.2 0.1 reshape.14.coarse_pos
  21.3 1.0 %reshape.17 = bf16[121,8,121]{0,2,1:T(8,128)(2,1)S(1)} reshape(bf16[121,968]{0,1:T(8,128)(2,1)} %param.10) | data formatting | bytes 468512 | tf_op jit(solution)/shard_map/reshape | solution.py:313
  22.3 0.2 copy.14
  22.5 0.1 pad.14.clone
  22.5 0.0 copy-start.2
  22.6 0.0 copy-start.1
  22.6 3.8 %copy-done.1 = bf16[121,38236]{0,1:T(8,128)(2,1)S(1)} copy-done((bf16[121,38236]{0,1:T(8,128)(2,1)S(1)}, bf16[121,38236]{0,1:T(8,128)(2,1)}, u32[]{:S(2)}) %copy-start.1) | copy-done | bytes 9253136
  26.4 4.3 %shard_map.74.operators.stored_operators = bf16[128,40960]{1,0:T(8,128)(2,1)S(1)} custom-call(bf16[38236,121]{1,0:T(8,128)(2,1)S(1)} %bitcast.14), custom_call_target="tpu_custom_call" | custom-call | bytes 41943040 | tf_op jit(solution)/shard_map/pallas_call | solution.py:355
  30.7 0.0 copy-done.2
  30.7 9.7 %shard_map.75.local_sum = f32[128,256]{1,0:T(8,128)S(1)} custom-call(s32[1]{0:T(128)} %bitcast.core_ref, bf16[128,128]{1,0:T(8,128)(2,1)S(1)} %pad.13.local_cells, s32[316,256]{1,0:T(8,128)S(1)} %copy-done.2, bf16[128,40960]{1,0:T(8,128)(2,1)S(1)} %shard_map.74.operators.stored_operators), custom_call_target="tpu_custom_call" | custom-call | bytes 31457280 | tf_op jit(solution)/shard_map/pallas_call | solution.py:429
  40.4 0.0 copy-start
  40.4 4.0 %copy-done = bf16[128,40960]{1,0:T(8,128)(2,1)} copy-done((bf16[128,40960]{1,0:T(8,128)(2,1)}, bf16[128,40960]{1,0:T(8,128)(2,1)S(1)}, u32[]{:S(2)}) %copy-start) | copy-done | bytes 10485784
  44.4 2.3 %all-to-all-done.arrived = bf16[128,32,128]{2,1,0:T(8,128)(2,1)S(1)} async-done(((bf16[128,32,128]{2,1,0:T(8,128)(2,1)}), bf16[128,32,128]{2,1,0:T(8,128)(2,1)S(1)}, u32[]{:S(2)}, u32[]{:S(2)}) %all-to-all-start) | async-done | bytes 1048608 | tf_op jit(solution)/shard_map/all_to_all | solution.py:424
  46.7 24.4 %shard_map.76 = (f32[128,128]{1,0:T(8,128)S(1)}, f32[128,128]{1,0:T(8,128)S(1)}) custom-call(s32[1]{0:T(128)} %bitcast.core_ref, s32[10240]{0:T(1024)S(1)} %reshape.14.coarse_pos, bf16[128,32,128]{2,1,0:T(8,128)(2,1)S(1)} %all-to-all-done.arrived, s32[316,256]{1,0:T(8,128)S(1)} %copy-done.2, f32[128,256]{1,0:T(8,128)S(1)} %shard_map.75.local_sum, ...), custom_call_target="tpu_custom_call" | custom-call | tf_op jit(solution)/shard_map/pallas_call | solution.py:456
  71.0 3.7 %collective-permute-start = (f32[128,128]{1,0:T(8,128)S(1)}, f32[128,128]{1,0:T(8,128)S(1)}, u32[]{:S(2)}, u32[]{:S(2)}) collective-permute-start(f32[128,128]{1,0:T(8,128)S(1)} %get-tuple-element.8), channel_id=1, source_target_pairs={{0,1},{1,0},{2,3},{3,2},{4,5},{5,4},{6,7},{7,6},{8,9},{9,8},{10,11... | collective-permute-start | bytes 196616 | tf_op jit(solution)/shard_map/ppermute | solution.py:475
  74.7 0.9 %collective-permute-done = f32[128,128]{1,0:T(8,128)S(1)} collective-permute-done((f32[128,128]{1,0:T(8,128)S(1)}, f32[128,128]{1,0:T(8,128)S(1)}, u32[]{:S(2)}, u32[]{:S(2)}) %collective-permute-start) | collective-permute-done | bytes 65568 | tf_op jit(solution)/shard_map/ppermute | solution.py:475
  75.6 0.6 slice_add_fusion
  (2 shorter events, 0.1 us)
Async XLA Ops:
  3.0 43.6 %all-to-all-start = ((bf16[128,32,128]{2,1,0:T(8,128)(2,1)}), bf16[128,32,128]{2,1,0:T(8,128)(2,1)S(1)}, u32[]{:S(2)}, u32[]{:S(2)}) async-start(bf16[128,32,128]{2,1,0:T(8,128)(2,1)} %shard_map.73), calls=%async_computation | async-start | bytes 2097152 | tf_op jit(solution)/shard_map/all_to_all | solution.py:424
  22.5 8.2 %copy-start.2 = (s32[316,256]{1,0:T(8,128)S(1)}, s32[316,256]{1,0:T(8,128)}, u32[]{:S(2)}) copy-start(s32[316,256]{1,0:T(8,128)} %pairs.3) | copy-start | bytes 970756
  22.6 3.8 %copy-start.1 = (bf16[121,38236]{0,1:T(8,128)(2,1)S(1)}, bf16[121,38236]{0,1:T(8,128)(2,1)}, u32[]{:S(2)}) copy-start(bf16[121,38236]{0,1:T(8,128)(2,1)} %param.9) | copy-start | bytes 27759340
  40.4 4.0 %copy-start = (bf16[128,40960]{1,0:T(8,128)(2,1)}, bf16[128,40960]{1,0:T(8,128)(2,1)S(1)}, u32[]{:S(2)}) copy-start(bf16[128,40960]{1,0:T(8,128)(2,1)S(1)} %shard_map.74.operators.stored_operators) | copy-start | bytes 31457284
  71.0 4.6 %collective-permute-start = (f32[128,128]{1,0:T(8,128)S(1)}, f32[128,128]{1,0:T(8,128)S(1)}, u32[]{:S(2)}, u32[]{:S(2)}) collective-permute-start(f32[128,128]{1,0:T(8,128)S(1)} %get-tuple-element.8), channel_id=1, source_target_pairs={{0,1},{1,0},{2,3},{3,2},{4,5},{5,4},{6,7},{7,6},{8,9},{9,8},{10,11... | collective-permute-start | bytes 196616 | tf_op jit(solution)/shard_map/ppermute | solution.py:475

commit v4 on v3

--- a/solution.py
+++ b/solution.py
@@ -17,6 +17,7 @@
 HALF = 256
 FETCHES = 4
 SPAN = 8
+COARSE_SPAN = 8
 BY_PRODUCT = (0, 3, 6, 8, 11, 14)
 BLOCK = 128
 
@@ -171,13 +172,9 @@
             blocks.append(jnp.concatenate(lines, axis=0))
         return jnp.concatenate(blocks, axis=1).astype(BF)
 
-    def operator_pair(group, pair):
-        start = pl.multiple_of((group * GROUP + 2 * pair) * width, 2 * width)
-        return operators[:, pl.ds(start, 2 * width)]
-
-    def operator_span(group, pair):
-        start = pl.multiple_of((group * GROUP + 2 * pair) * width, 2 * width)
-        return operators[:, pl.ds(start, 2 * SPAN * width)]
+    def operator_span(group, done, count):
+        start = pl.multiple_of((group * GROUP + done) * width, 2 * width)
+        return operators[:, pl.ds(start, count * width)]
 
     def near_step(table, tile, group, base, gather_now=True):
         if gather_now:
@@ -187,7 +184,7 @@
             here = slice(2 * pair * width, 2 * (pair + SPAN) * width)
             ready = jnp.maximum(group - 1, 0)
             if pair % SPAN == 0:
-                total = total + dot(operator_span(ready, pair), cells[here, :])
+                total = total + dot(operator_span(ready, 2 * pair, 2 * SPAN), cells[here, :])
             if gather_now:
                 for c in (2 * pair, 2 * pair + 1):
                     row = position[c : c + 1]
@@ -200,18 +197,18 @@
         total = coarse_sum[...]
         ready = jnp.maximum(group - 1, 0)
         base = group * (GROUP * coarse_targets)
-        for pair in range(GROUP // 2):
-            at = 2 * pair * coarse_targets
+        for done in range(0, GROUP, COARSE_SPAN):
+            at = done * coarse_targets
             both = jnp.concatenate(
                 [
                     picked[at + j * coarse_targets : at + (j + 1) * coarse_targets, :].astype(BF)
-                    for j in range(2)
+                    for j in range(COARSE_SPAN)
                 ],
                 axis=1,
             )
-            total = total + nt_dot(operator_pair(ready, pair), both)
+            total = total + nt_dot(operator_span(ready, done, COARSE_SPAN), both)
             if gather_now:
-                for row in range(at, at + 2 * coarse_targets):
+                for row in range(at, at + COARSE_SPAN * coarse_targets):
                     picked[pl.ds(row, 1), :] = coarse_rows[pl.ds(coarse_pos[base + row], 1), :]
         coarse_sum[...] = total
 

time: 76.6 us -> 75.4 us (0.984)
  Pallas kernels: 41.4 us -> 40.2 us
    pallas_call x1, Pallas kernels: 24.4 us -> 23.2 us  [per_device(): pl.pallas_call(functools.partial(main_kernel, order_terms), out_shape=(ha...]
  transfers between devices with their start and end apart: 2 -> 2, of which waited for: 2 -> 2; matrix products, arithmetic and copies ran while one was open for 4% -> 4% of each run, Pallas kernels for 18% -> 19%
where the time goes in v4:
time: 75.4 us; the launch traced here: 75 us
  Pallas kernels  40.2 us (53%)
  starting transfers between devices  20 us (27%)
  local copies, waits for them, and re-layouts  10 us (13%)
  waiting for transfers between devices  3.18 us (4%)
  other arithmetic  1.53 us (2%)
    pallas_call x1, Pallas kernels, per_device(): pl.pallas_call(functools.partial(main_kernel, order_terms), out_shape=(ha...  23.2 us
    all_to_all x1, starting transfers between devices, per_device(): lax.all_to_all(outgoing, 'leaf', split_axis=0, concat_axis=0, tiled=True)  16.3 us
    pallas_call x1, Pallas kernels, per_device(): pl.pallas_call(local_kernel, out_shape=jax.ShapeDtypeStruct((WIDTH, targe...  9.72 us
    unnamed x9, local copies, waits for them, and re-layouts  8.1 us
    pallas_call x1, Pallas kernels, arrange_classes(): pl.pallas_call(functools.partial(arrange_kernel, class_count), out_shape=...  4.28 us
    ppermute x1, starting transfers between devices, per_device(): other = lax.ppermute(send, 'top', [(0, 1), (1, 0)])  3.64 us
    pallas_call x1, Pallas kernels, per_device(): pl.pallas_call(outgoing_kernel, out_shape=jax.ShapeDtypeStruct((peers, sl...  3.02 us
    all_to_all x1, waiting for transfers between devices, per_device(): lax.all_to_all(outgoing, 'leaf', split_axis=0, concat_axis=0, tiled=True)  2.28 us
  transfers between devices with their start and end apart: 2, of which 2 were waited for; matrix products, arithmetic and copies ran while one was open for 4% of the time, Pallas kernels for 19%

profile of v4, /device:TPU:1, one launch (start us, length us, event | category | flops | bytes accessed | tf_op | source)
XLA Modules:
  0.0 75.0 jit_solution(9995108226883671657)
XLA Ops:
  0.0 3.0 %shard_map.73 = bf16[128,32,128]{2,1,0:T(8,128)(2,1)} custom-call(bf16[121,128]{1,0:T(8,128)(2,1)} %cells.1, s32[16,128]{1,0:T(8,128)} %bitcast.19, bf16[968,121]{1,0:T(8,128)(2,1)} %bitcast.18), custom_call_target="tpu_custom_call" | custom-call | tf_op jit(solution)/shard_map/pallas_call | solution.py:406
  3.0 16.3 %all-to-all-start = ((bf16[128,32,128]{2,1,0:T(8,128)(2,1)}), bf16[128,32,128]{2,1,0:T(8,128)(2,1)S(1)}, u32[]{:S(2)}, u32[]{:S(2)}) async-start(bf16[128,32,128]{2,1,0:T(8,128)(2,1)} %shard_map.73), calls=%async_computation | async-start | bytes 2097152 | tf_op jit(solution)/shard_map/all_to_all | solution.py:421
  19.4 0.8 %pad.13.local_cells = bf16[128,128]{1,0:T(8,128)(2,1)S(1)} pad(bf16[121,128]{1,0:T(8,128)(2,1)} %cells.1, bf16[]{:T(256)} %constant.60.clone.1), padding=0_7x0_0 | pad | bytes 63746 | tf_op jit(solution)/shard_map/jit(_pad)/pad | solution.py:423
  20.1 0.9 %fusion.5 = s32[316,32]{0,1:T(8,128)S(1)} fusion(s32[316,32]{0,1:T(8,128)} %param.13, s32[]{:T(128)} %axis_index.12), kind=kLoop, calls=%fused_computation.18 | loop fusion | flops 465152 | bytes 80900 | tf_op jit(solution)/shard_map/jit(_where)/select_n | solution.py:446
  21.0 0.1 copy.13
  21.2 0.1 reshape.14.coarse_pos
  21.3 1.0 %reshape.17 = bf16[121,8,121]{0,2,1:T(8,128)(2,1)S(1)} reshape(bf16[121,968]{0,1:T(8,128)(2,1)} %param.10) | data formatting | bytes 468512 | tf_op jit(solution)/shard_map/reshape | solution.py:310
  22.3 0.2 copy.14
  22.5 0.1 pad.14.clone
  22.5 0.0 copy-start.2
  22.6 0.0 copy-start.1
  22.6 3.8 %copy-done.1 = bf16[121,38236]{0,1:T(8,128)(2,1)S(1)} copy-done((bf16[121,38236]{0,1:T(8,128)(2,1)S(1)}, bf16[121,38236]{0,1:T(8,128)(2,1)}, u32[]{:S(2)}) %copy-start.1) | copy-done | bytes 9253136
  26.4 4.3 %shard_map.74.operators.stored_operators = bf16[128,40960]{1,0:T(8,128)(2,1)S(1)} custom-call(bf16[38236,121]{1,0:T(8,128)(2,1)S(1)} %bitcast.14), custom_call_target="tpu_custom_call" | custom-call | bytes 41943040 | tf_op jit(solution)/shard_map/pallas_call | solution.py:352
  30.7 0.0 copy-done.2
  30.7 9.7 %shard_map.75.local_sum = f32[128,256]{1,0:T(8,128)S(1)} custom-call(s32[1]{0:T(128)} %bitcast.core_ref, bf16[128,128]{1,0:T(8,128)(2,1)S(1)} %pad.13.local_cells, s32[316,256]{1,0:T(8,128)S(1)} %copy-done.2, bf16[128,40960]{1,0:T(8,128)(2,1)S(1)} %shard_map.74.operators.stored_operators), custom_call_target="tpu_custom_call" | custom-call | bytes 31457280 | tf_op jit(solution)/shard_map/pallas_call | solution.py:426
  40.4 0.0 copy-start
  40.4 4.0 %copy-done = bf16[128,40960]{1,0:T(8,128)(2,1)} copy-done((bf16[128,40960]{1,0:T(8,128)(2,1)}, bf16[128,40960]{1,0:T(8,128)(2,1)S(1)}, u32[]{:S(2)}) %copy-start) | copy-done | bytes 10485784
  44.4 2.3 %all-to-all-done.arrived = bf16[128,32,128]{2,1,0:T(8,128)(2,1)S(1)} async-done(((bf16[128,32,128]{2,1,0:T(8,128)(2,1)}), bf16[128,32,128]{2,1,0:T(8,128)(2,1)S(1)}, u32[]{:S(2)}, u32[]{:S(2)}) %all-to-all-start) | async-done | bytes 1048608 | tf_op jit(solution)/shard_map/all_to_all | solution.py:421
  46.7 23.2 %shard_map.76 = (f32[128,128]{1,0:T(8,128)S(1)}, f32[128,128]{1,0:T(8,128)S(1)}) custom-call(s32[1]{0:T(128)} %bitcast.core_ref, s32[10240]{0:T(1024)S(1)} %reshape.14.coarse_pos, bf16[128,32,128]{2,1,0:T(8,128)(2,1)S(1)} %all-to-all-done.arrived, s32[316,256]{1,0:T(8,128)S(1)} %copy-done.2, f32[128,256]{1,0:T(8,128)S(1)} %shard_map.75.local_sum, ...), custom_call_target="tpu_custom_call" | custom-call | tf_op jit(solution)/shard_map/pallas_call | solution.py:453
  69.9 3.6 %collective-permute-start = (f32[128,128]{1,0:T(8,128)S(1)}, f32[128,128]{1,0:T(8,128)S(1)}, u32[]{:S(2)}, u32[]{:S(2)}) collective-permute-start(f32[128,128]{1,0:T(8,128)S(1)} %get-tuple-element.8), channel_id=1, source_target_pairs={{0,1},{1,0},{2,3},{3,2},{4,5},{5,4},{6,7},{7,6},{8,9},{9,8},{10,11... | collective-permute-start | bytes 196616 | tf_op jit(solution)/shard_map/ppermute | solution.py:472
  73.5 0.9 %collective-permute-done = f32[128,128]{1,0:T(8,128)S(1)} collective-permute-done((f32[128,128]{1,0:T(8,128)S(1)}, f32[128,128]{1,0:T(8,128)S(1)}, u32[]{:S(2)}, u32[]{:S(2)}) %collective-permute-start) | collective-permute-done | bytes 65568 | tf_op jit(solution)/shard_map/ppermute | solution.py:472
  74.4 0.6 slice_add_fusion
  (2 shorter events, 0.1 us)
Async XLA Ops:
  3.0 43.6 %all-to-all-start = ((bf16[128,32,128]{2,1,0:T(8,128)(2,1)}), bf16[128,32,128]{2,1,0:T(8,128)(2,1)S(1)}, u32[]{:S(2)}, u32[]{:S(2)}) async-start(bf16[128,32,128]{2,1,0:T(8,128)(2,1)} %shard_map.73), calls=%async_computation | async-start | bytes 2097152 | tf_op jit(solution)/shard_map/all_to_all | solution.py:421
  22.5 8.2 %copy-start.2 = (s32[316,256]{1,0:T(8,128)S(1)}, s32[316,256]{1,0:T(8,128)}, u32[]{:S(2)}) copy-start(s32[316,256]{1,0:T(8,128)} %pairs.3) | copy-start | bytes 970756
  22.6 3.8 %copy-start.1 = (bf16[121,38236]{0,1:T(8,128)(2,1)S(1)}, bf16[121,38236]{0,1:T(8,128)(2,1)}, u32[]{:S(2)}) copy-start(bf16[121,38236]{0,1:T(8,128)(2,1)} %param.9) | copy-start | bytes 27759340
  40.4 4.0 %copy-start = (bf16[128,40960]{1,0:T(8,128)(2,1)}, bf16[128,40960]{1,0:T(8,128)(2,1)S(1)}, u32[]{:S(2)}) copy-start(bf16[128,40960]{1,0:T(8,128)(2,1)S(1)} %shard_map.74.operators.stored_operators) | copy-start | bytes 31457284
  69.9 4.5 %collective-permute-start = (f32[128,128]{1,0:T(8,128)S(1)}, f32[128,128]{1,0:T(8,128)S(1)}, u32[]{:S(2)}, u32[]{:S(2)}) collective-permute-start(f32[128,128]{1,0:T(8,128)S(1)} %get-tuple-element.8), channel_id=1, source_target_pairs={{0,1},{1,0},{2,3},{3,2},{4,5},{5,4},{6,7},{7,6},{8,9},{9,8},{10,11... | collective-permute-start | bytes 196616 | tf_op jit(solution)/shard_map/ppermute | solution.py:472
